TPU v7x, 128 devices: a whole 4x4x4 slice. The times are simulated.
128 devices in a mesh: px: 8 (over y, core), py: 16 (over x, z).
Axes of the slice: x: 4, y: 4, z: 4, core: 2. Of those that a mesh axis runs over, the one named last changes fastest.
Arguments:
- coupling_vals: float32 [32, 64, 9, 64, 64], P('px', 'py'), may hold values from -0.75 to 0.75
- coupling_cols: int32 [32, 64, 9], P('px', 'py'), may hold values from 0 to 2047, as said below
- coupling_len: int32 [32, 64], P('px', 'py'), may hold values from 1 to 9
- interp_vals: float32 [32, 64, 4, 64, 64], P('px', 'py'), may hold values from -0.75 to 0.75
- interp_cols: int32 [32, 64, 4], P('px', 'py'), may hold values from 0 to 511, as said below
- interp_len: int32 [32, 64], P('px', 'py'), may hold values from 1 to 4
- owner_map: int32 [8, 16, 4, 1], P('px'), may hold values from 0 to 15; in each aligned block of 4 rows (0 to 3, 4 to 7, ..., all dimensions but the last counted through in order) at most 2 rows name the same one
Outputs:
- relayed_rows: float32 [4096, 25, 64, 64], P(('px', 'py'))
- relayed_ids: int32 [4096], P(('px', 'py'))
Inputs may be any that keep to these rules, and one draw needn't show every extreme that they name: `coupling_cols`: row (x, y) names in its first coupling_len[x, y] slots distinct fine blocks x' 64 + y' of the grid with x' - x and y' - y each in -1, 0, 1; later slots name the row's own block. `interp_cols`: row (x, y) names in its first interp_len[x, y] slots distinct coarse blocks X 32 + Y of the coarse grid with X - x div 2 and Y - y div 2 each 0 or 1; later slots name (x div 2) * 32 + y div 2. `owner_map`: among the 4 entries of one grid device, no value appears more than 2 times.
All inputs are finite; a program needn't handle non-finite values.
Results may differ from a plain program's by a relative error of at most 0.0003.
Values sent between devices are 32-bit elements; how exact they have to be, the bound alone decides.
No kernel may reach another device: no remote copies, remote signals or barrier semaphores. Data moves between devices by JAX's collectives and lax.ppermute only.
A program may use at most 256 MiB of HBM per device.

v0:
```python
import jax
import jax.numpy as jnp
from jax import lax
from jax.sharding import PartitionSpec as P

CAP = 2


def extended(cells, sides, width):
    for axis, dim in sides:
        count = lax.axis_size(axis)
        ends = count - 1
        head = lax.slice_in_dim(cells, 0, width, axis=dim)
        tail = lax.slice_in_dim(cells, cells.shape[dim] - width, cells.shape[dim], axis=dim)
        cells = jnp.concatenate(
            [
                lax.ppermute(tail, axis, [(i, (i + 1) % count) for i in range(ends)]),
                cells,
                lax.ppermute(head, axis, [((i + 1) % count, i) for i in range(ends)]),
            ],
            axis=dim,
        )
    return cells


def fold_pairs(parity_x, parity_y):
    pairs = []
    for offset in range(9):
        step_x = offset // 3 - 1
        step_y = offset % 3 - 1
        for corner in range(4):
            target_x = (parity_x + step_x) // 2 + corner // 2 + 1
            target_y = (parity_y + step_y) // 2 + corner % 2 + 1
            pairs.append((offset, corner, target_x * 4 + target_y))
    return pairs


def place_slots(values, offset, lengths, count):
    slot_ids = jnp.arange(count, dtype=jnp.int32)
    live = slot_ids < lengths[:, :, None]
    match = ((offset[..., None] == slot_ids) & live[..., None]).astype(jnp.int32)
    present = jnp.sum(match, axis=2) > 0
    picked = jnp.argmax(match, axis=2)
    gathered = jnp.take_along_axis(values, picked[:, :, :, None, None], axis=2)
    return jnp.where(present[:, :, :, None, None], gathered, jnp.zeros_like(gathered))


def dense_coupling(values, columns, lengths, row_x, row_y, fine_y):
    column_x = columns // fine_y
    column_y = columns % fine_y
    offset = (column_x - row_x + 1) * 3 + (column_y - row_y + 1)
    return place_slots(values, offset, lengths, 9)


def dense_interp(values, columns, lengths, row_x, row_y, coarse_y):
    offset = (columns // coarse_y - row_x // 2) * 2 + (columns % coarse_y - row_y // 2)
    return place_slots(values, offset, lengths, 4)


def galerkin_terms(operator_blocks, interp_cycle):
    span_x = operator_blocks.shape[0] // 2
    span_y = operator_blocks.shape[1] // 2
    width = operator_blocks.shape[-1]
    merged_list = []
    own_list = []
    for parity_x in (0, 1):
        for parity_y in (0, 1):
            fine_rows = operator_blocks[parity_x::2, parity_y::2]
            pieces = []
            for step_x in (-1, 0, 1):
                for step_y in (-1, 0, 1):
                    begin_x = 1 + parity_x + step_x
                    begin_y = 1 + parity_y + step_y
                    pieces.append(
                        interp_cycle[
                            begin_x : begin_x + 2 * span_x : 2, begin_y : begin_y + 2 * span_y : 2
                        ]
                    )
            targets = [None] * 16
            for offset, corner, target in fold_pairs(parity_x, parity_y):
                product = jnp.einsum(
                    "xyab,xybd->xyad",
                    fine_rows[:, :, offset],
                    pieces[offset][:, :, corner],
                    precision=lax.Precision.HIGHEST,
                )
                targets[target] = product if targets[target] is None else targets[target] + product
            filled = [
                t if t is not None else jnp.zeros((span_x, span_y, width, width), jnp.float32)
                for t in targets
            ]
            merged_list.append(jnp.stack(filled, axis=2))
            own_list.append(
                interp_cycle[
                    1 + parity_x : 1 + parity_x + 2 * span_x : 2,
                    1 + parity_y : 1 + parity_y + 2 * span_y : 2,
                ]
            )
    blocks = jnp.einsum(
        "kxypba,kxynbc->xypnac",
        jnp.stack(own_list),
        jnp.stack(merged_list),
        precision=lax.Precision.HIGHEST,
    )
    accumulated = jnp.zeros((span_x + 1, span_y + 1, 25, width, width), blocks.dtype)
    for corner in range(4):
        high_x = corner // 2
        high_y = corner % 2
        placed = blocks[:, :, corner].reshape(span_x, span_y, 4, 4, width, width)
        placed = jnp.pad(
            placed,
            (
                (high_x, 1 - high_x),
                (high_y, 1 - high_y),
                (1 - high_x, high_x),
                (1 - high_y, high_y),
                (0, 0),
                (0, 0),
            ),
        )
        accumulated = accumulated + placed.reshape(span_x + 1, span_y + 1, 25, width, width)
    return accumulated


def body(
    coupling_vals, coupling_cols, coupling_len, interp_vals, interp_cols, interp_len, owner_map
):
    block_x = coupling_cols.shape[0]
    block_y = coupling_cols.shape[1]
    span_x = block_x // 2
    span_y = block_y // 2
    width = coupling_vals.shape[-1]
    peers = lax.axis_size("py")
    fine_y = block_y * peers
    coarse_y = fine_y // 2
    mine_x = lax.axis_index("px")
    mine_y = lax.axis_index("py")
    row_x = mine_x * block_x + jnp.arange(block_x, dtype=jnp.int32)[:, None, None]
    row_y = mine_y * block_y + jnp.arange(block_y, dtype=jnp.int32)[None, :, None]
    operator_blocks = dense_coupling(
        coupling_vals, coupling_cols, coupling_len, row_x, row_y, fine_y
    )
    interp_blocks = dense_interp(interp_vals, interp_cols, interp_len, row_x, row_y, coarse_y)
    joined = jnp.concatenate([operator_blocks, interp_blocks], axis=2)
    margin = extended(joined, (("px", 0), ("py", 1)), 3)
    terms = galerkin_terms(margin[1 : block_x + 3, 1 : block_y + 3, :9], margin[:, :, 9:])
    coarse_own = terms[1 : span_x + 1, 1 : span_y + 1]
    per_device = span_x * span_y
    own_rows = coarse_own.reshape(per_device, 25 * width * width)
    target_all = owner_map[0, :, :, 0]
    target = lax.dynamic_index_in_dim(target_all, mine_y, 0, keepdims=False)
    hits = (target[:, None] == jnp.arange(peers, dtype=jnp.int32)).astype(jnp.int32)
    rank = jnp.sum((jnp.cumsum(hits, axis=0) - hits) * hits, axis=-1)
    slot = target * CAP + rank
    place = (slot[:, None] == jnp.arange(peers * CAP, dtype=jnp.int32)).astype(jnp.float32)
    outgoing = jnp.einsum("ks,kv->sv", place, own_rows, precision=lax.Precision.HIGHEST)
    outgoing = outgoing.reshape(peers, CAP, 25, width, width)
    incoming = lax.all_to_all(outgoing, "py", split_axis=0, concat_axis=0, tiled=True)
    relayed_rows = incoming.reshape(peers * CAP, 25, width, width)
    arrive = (target_all == mine_y).astype(jnp.int32)
    order_in = jnp.cumsum(arrive, axis=1) - arrive
    local = jnp.arange(per_device, dtype=jnp.int32)[None, :]
    sender = jnp.arange(peers, dtype=jnp.int32)[:, None]
    ident = (mine_x * span_x + local // span_y) * coarse_y + sender * span_y + local % span_y
    match = arrive[:, :, None] * (order_in[:, :, None] == jnp.arange(CAP, dtype=jnp.int32)).astype(
        jnp.int32
    )
    present = jnp.sum(match, axis=1)
    found = jnp.sum(match * ident[:, :, None], axis=1)
    relayed_ids = jnp.where(present > 0, found, -1).reshape(peers * CAP)
    return (relayed_rows, relayed_ids)


def solution(mesh):
    in_specs = (
        P("px", "py", None, None, None),
        P("px", "py", None),
        P("px", "py"),
        P("px", "py", None, None, None),
        P("px", "py", None),
        P("px", "py"),
        P("px", None, None, None),
    )
    out_specs = (P(("px", "py"), None, None, None), P(("px", "py")))
    return jax.shard_map(body, mesh=mesh, in_specs=in_specs, out_specs=out_specs, check_vma=False)
```

profile of v0, /device:TPU:84, one launch (start us, length us, event | category | flops | bytes accessed | tf_op | source)
XLA Modules:
  0.0 1174.1 jit_solution(14221024734071285680)
XLA Ops:
  6.6 6.9 gather_fusion
  23.1 3.6 collective-permute-start.1
  26.8 54.1 %collective-permute-done = f32[3,4,13,64,64]{4,3,1,0,2:T(8,128)S(1)} collective-permute-done((f32[3,4,13,64,64]{4,3,1,0,2:T(8,128)S(1)}, f32[3,4,13,64,64]{4,3,1,0,2:T(8,128)S(1)}, u32[]{:S(2)}, u32[]{:S(2)}) %collective-permute-start) | collective-permute-done | bytes 2555936 | tf_op jit(solution)/shard_map/ppermute | solution.py:17
  83.2 5.3 pad_maximum_fusion
  88.5 9.5 fusion.109
  98.0 3.5 collective-permute-start.2
  108.3 269.3 %collective-permute-done.2 = f32[10,3,13,64,64]{4,3,1,0,2:T(8,128)} collective-permute-done((f32[10,3,13,64,64]{4,3,1,0,2:T(8,128)}, f32[10,3,13,64,64]{4,3,1,0,2:T(8,128)}, u32[]{:S(2)}, u32[]{:S(2)}) %collective-permute-start.2) | collective-permute-done | bytes 6389792 | tf_op jit(solution)/shard_map/ppermute | solution.py:17
  377.5 10.9 pad_maximum_fusion.6
  388.5 8.1 fusion.110
  396.6 11.8 %pad_maximum_fusion.1 = f32[10,10,4,64,64]{4,3,1,0,2:T(8,128)} fusion(f32[10,3,13,64,64]{4,3,1,0,2:T(8,128)} %collective-permute-done.3, f32[10,3,13,64,64]{4,3,1,0,2:T(8,128)} %collective-permute-done.2, f32[3,4,13,64,64]{4,3,1,0,2:T(8,128)} %collective-permute-done.1, f32[3,4,13,64,64]{4,3,1,0,2:T(8,128)} %copy-done.8, ...), kind=kLoop, calls=%fused_computation.11 | loop fusion | flops 8192000 | bytes 27852800 | tf_op jit(solution)/shard_map/concatenate | solution.py:15
  408.4 13.0 %slice_bitcast_fusion.391 = (f32[1,3,3,4,64,64]{5,4,2,1,3,0:T(8,128)}, f32[1,3,3,4,64,64]{5,4,2,1,3,0:T(8,128)}, f32[1,3,3,4,64,64]{5,4,2,1,3,0:T(8,128)}, f32[1...) fusion(f32[10,10,4,64,64]{4,3,1,0,2:T(8,128)} %pad_maximum_fusion.1), kind=kLoop, calls=%fused_computation.446 | loop fusion | bytes 20054016 | tf_op jit(solution)/shard_map/stack | solution.py:101
  750.8 25.1 %fusion.7 = f32[3,3,4,16,64,64]{4,5,2,3,1,0:T(8,128)} fusion(f32[1,3,3,16,64,64]{4,5,0,3,2,1:T(8,128)} %bitcast.148, f32[1,3,3,16,64,64]{4,5,0,3,2,1:T(8,128)} %bitcast.647, f32[1,3,3,16,64,64]{4,5,0,3,2,1:T(8,128)} %bitcast.652, f32[1,3,3,16,64,64]{4,5,0,3,2,1:T(8,128)} %bitcast.651, f32[1,3,3,4,64,64]{5,4,2,1,3,0:T(8,128)S(1)} %copy-done.23, ...), kind=kOutput, calls=%fused_computation.21 | convolution fusion | flops 7256604672 | bytes 21233664 | tf_op jit(solution)/shard_map/kxypba,kxynbc->xypnac/dot_general | solution.py:99
  775.9 10.0 fusion.108
  785.9 8.4 pad_add_fusion
  794.3 14.0 %copy.204 = f32[4,4,5,5,64,64]{5,4,3,2,1,0:T(8,128)} copy(f32[4,4,5,5,64,64]{4,5,3,2,1,0:T(8,128)} %pad_add_fusion) | data formatting | bytes 13107200 | tf_op jit(solution)/shard_map/add | solution.py:121
  808.2 4.1 slice.851
  815.5 3.3 dot_general.588
  818.8 13.5 %fusion.11 = f32[16,2,25,64,64]{4,0,3,2,1:T(8,128)S(1)} fusion(f32[25,64,64,4]{2,1,0,3:T(8,128)} %dot_general.588, s32[16,2]{0,1:T(2,128)S(1)} %multiply_add_fusion, s32[4]{0:T(128)S(1)} %multiply_add_fusion.1), kind=kOutput, calls=%fused_computation.30 | convolution fusion | flops 157286528 | bytes 14745744 | tf_op jit(solution)/shard_map/ks,kv->sv/dot_general | solution.py:156
  832.3 12.2 %copy.206 = f32[16,2,25,64,64]{4,3,2,1,0:T(8,128)} copy(f32[16,2,25,64,64]{4,0,3,2,1:T(8,128)S(1)} %fusion.11) | data formatting | bytes 26214400 | tf_op jit(solution)/shard_map/ks,kv->sv/dot_general | solution.py:156
  844.4 24.5 %reshape.348 = f32[16,1,204800]{2,1,0:T(1,128)} reshape(f32[16,2,25,64,64]{4,3,2,1,0:T(8,128)} %copy.206) | data formatting | bytes 26214400
  868.9 8.0 all-to-all-start
  877.8 229.4 %all-to-all-done = f32[16,1,204800]{2,1,0:T(1,128)} async-done(((f32[16,1,204800]{2,1,0:T(1,128)}), f32[16,1,204800]{2,1,0:T(1,128)}, u32[]{:S(2)}, u32[]{:S(2)}) %all-to-all-start) | async-done | bytes 13107232 | tf_op jit(solution)/shard_map/all_to_all | solution.py:158
  1107.7 39.9 %reduce.40 = f32[16,204800]{1,0:T(8,128)} reduce(f32[16,1,204800]{2,1,0:T(1,128)} %all-to-all-done, f32[]{:T(128)} %broadcast.456), dimensions={1}, to_apply=%all_to_all.3.reduce_sub_computation | reduce | bytes 26214404 | tf_op jit(solution)/shard_map/all_to_all | solution.py:158
  1147.6 26.0 %reshape.349 = f32[16,2,25,64,64]{4,3,2,1,0:T(8,128)} reshape(f32[16,204800]{1,0:T(8,128)} %reduce.40) | data formatting | bytes 26214400
  (367 shorter events, 357.6 us)
Async XLA Ops:
  0.6 12.8 %copy-start = (f32[4,4,4,64,64]{4,3,2,1,0:T(8,128)S(1)}, f32[4,4,4,64,64]{4,3,2,1,0:T(8,128)}, u32[]{:S(2)}) copy-start(f32[4,4,4,64,64]{4,3,2,1,0:T(8,128)} %param.10) | copy-start | bytes 3145732
  18.6 64.6 %copy-start.2 = (f32[4,4,9,64,64]{4,3,1,0,2:T(8,128)}, f32[4,4,9,64,64]{4,3,1,0,2:T(8,128)S(1)}, u32[]{:S(2)}) copy-start(f32[4,4,9,64,64]{4,3,1,0,2:T(8,128)S(1)} %fusion.10) | copy-start | bytes 7077892
  21.2 59.7 %collective-permute-start = (f32[3,4,13,64,64]{4,3,1,0,2:T(8,128)S(1)}, f32[3,4,13,64,64]{4,3,1,0,2:T(8,128)S(1)}, u32[]{:S(2)}, u32[]{:S(2)}) collective-permute-start(f32[3,4,13,64,64]{4,3,1,0,2:T(8,128)S(1)} %get-tuple-element.37), channel_id=1, source_target_pairs={{0,16},{16,32},{32,48},{48,64},{64,80},{80,96},{96,112},{1,17},{17... | collective-permute-start | bytes 7667720 | tf_op jit(solution)/shard_map/ppermute | solution.py:17
  23.1 60.1 %collective-permute-start.1 = (f32[3,4,13,64,64]{4,3,1,0,2:T(8,128)S(1)}, f32[3,4,13,64,64]{4,3,1,0,2:T(8,128)}, u32[]{:S(2)}, u32[]{:S(2)}) collective-permute-start(f32[3,4,13,64,64]{4,3,1,0,2:T(8,128)S(1)} %get-tuple-element.38), channel_id=1, source_target_pairs={{16,0},{32,16},{48,32},{64,48},{80,64},{96,80},{112,96},{17,1},{33... | collective-permute-start | bytes 7667720 | tf_op jit(solution)/shard_map/ppermute | solution.py:19
  88.5 15.3 %copy-start.42 = (s32[1,16,4,1]{1,3,2,0:T(1,128)S(1)}, s32[1,16,4,1]{1,3,2,0:T(1,128)}, u32[]{:S(2)}) copy-start(s32[1,16,4,1]{1,3,2,0:T(1,128)} %param.13) | copy-start | bytes 772
  98.0 279.5 %collective-permute-start.2 = (f32[10,3,13,64,64]{4,3,1,0,2:T(8,128)}, f32[10,3,13,64,64]{4,3,1,0,2:T(8,128)}, u32[]{:S(2)}, u32[]{:S(2)}) collective-permute-start(f32[10,3,13,64,64]{4,3,1,0,2:T(8,128)} %get-tuple-element.12), channel_id=1, source_target_pairs={{0,1},{1,2},{2,3},{3,4},{4,5},{5,6},{6,7},{7,8},{8,9},{9,10},{10,1... | collective-permute-start | bytes 19169288 | tf_op jit(solution)/shard_map/ppermute | solution.py:17
  101.5 295.1 %collective-permute-start.3 = (f32[10,3,13,64,64]{4,3,1,0,2:T(8,128)}, f32[10,3,13,64,64]{4,3,1,0,2:T(8,128)}, u32[]{:S(2)}, u32[]{:S(2)}) collective-permute-start(f32[10,3,13,64,64]{4,3,1,0,2:T(8,128)} %get-tuple-element.13), channel_id=1, source_target_pairs={{1,0},{2,1},{3,2},{4,3},{5,4},{6,5},{7,6},{8,7},{9,8},{10,9},{11,1... | collective-permute-start | bytes 19169288 | tf_op jit(solution)/shard_map/ppermute | solution.py:19
  107.1 289.5 %slice-start = ((s8[4718592]{0:T(1024)(128)(4,1)}), s8[4194304]{0:T(1024)(128)(4,1)S(1)}, s32[]{:S(2)}) async-start(s8[4718592]{0:T(1024)(128)(4,1)} %bitcast.636), calls=%async_computation.1 | async-start | bytes 8388608
  108.3 288.3 %slice-start.1 = ((s8[4718592]{0:T(1024)(128)(4,1)}), s8[524288]{0:T(1024)(128)(4,1)S(1)}, s32[]{:S(2)}) async-start(s8[4718592]{0:T(1024)(128)(4,1)} %bitcast.636), calls=%async_computation.2 | async-start | bytes 1048576
  396.6 50.3 %copy-start.4 = (f32[3,3,9,64,64]{4,3,1,0,2:T(8,128)}, f32[3,3,9,64,64]{4,3,1,0,2:T(8,128)S(1)}, u32[]{:S(2)}) copy-start(f32[3,3,9,64,64]{4,3,1,0,2:T(8,128)S(1)} %get-tuple-element.34) | copy-start | bytes 3981316
  396.6 59.1 %copy-start.3 = (f32[3,3,9,64,64]{4,3,1,0,2:T(8,128)}, f32[3,3,9,64,64]{4,3,1,0,2:T(8,128)S(1)}, u32[]{:S(2)}) copy-start(f32[3,3,9,64,64]{4,3,1,0,2:T(8,128)S(1)} %get-tuple-element.36) | copy-start | bytes 3981316
  408.4 13.0 %copy-start.6 = (f32[3,3,9,64,64]{4,3,1,0,2:T(8,128)S(1)}, f32[3,3,9,64,64]{4,3,1,0,2:T(8,128)}, u32[]{:S(2)}) copy-start(f32[3,3,9,64,64]{4,3,1,0,2:T(8,128)} %get-tuple-element.33) | copy-start | bytes 3981316
  421.4 12.8 %copy-start.12 = (f32[3,3,4,64,64]{4,3,1,0,2:T(8,128)}, f32[3,3,4,64,64]{4,3,1,0,2:T(8,128)S(1)}, u32[]{:S(2)}) copy-start(f32[3,3,4,64,64]{4,3,1,0,2:T(8,128)S(1)} %get-tuple-element.30) | copy-start | bytes 1769476
  421.4 35.1 %copy-start.11 = (f32[3,3,4,64,64]{4,3,1,0,2:T(8,128)}, f32[3,3,4,64,64]{4,3,1,0,2:T(8,128)S(1)}, u32[]{:S(2)}) copy-start(f32[3,3,4,64,64]{4,3,1,0,2:T(8,128)S(1)} %get-tuple-element.25) | copy-start | bytes 1769476
  421.4 35.5 %copy-start.9 = (f32[3,3,4,64,64]{4,3,1,0,2:T(8,128)}, f32[3,3,4,64,64]{4,3,1,0,2:T(8,128)S(1)}, u32[]{:S(2)}) copy-start(f32[3,3,4,64,64]{4,3,1,0,2:T(8,128)S(1)} %get-tuple-element.24) | copy-start | bytes 1769476
  515.9 12.9 %copy-start.31 = (f32[3,3,1,64,64]{3,4,2,1,0:T(8,128)S(1)}, f32[3,3,1,64,64]{3,4,2,1,0:T(8,128)}, u32[]{:S(2)}) copy-start(f32[3,3,1,64,64]{3,4,2,1,0:T(8,128)} %copy.172) | copy-start | bytes 442372
  593.8 12.9 %copy-start.37 = (f32[3,3,1,64,64]{3,4,2,1,0:T(8,128)S(1)}, f32[3,3,1,64,64]{3,4,2,1,0:T(8,128)}, u32[]{:S(2)}) copy-start(f32[3,3,1,64,64]{3,4,2,1,0:T(8,128)} %copy.179) | copy-start | bytes 442372
  593.8 13.6 %copy-start.34 = (f32[3,3,1,64,64]{3,4,2,1,0:T(8,128)S(1)}, f32[3,3,1,64,64]{3,4,2,1,0:T(8,128)}, u32[]{:S(2)}) copy-start(f32[3,3,1,64,64]{3,4,2,1,0:T(8,128)} %copy.180) | copy-start | bytes 442372
  595.6 12.6 %copy-start.29 = (f32[3,3,1,64,64]{3,4,2,1,0:T(8,128)S(1)}, f32[3,3,1,64,64]{3,4,2,1,0:T(8,128)}, u32[]{:S(2)}) copy-start(f32[3,3,1,64,64]{3,4,2,1,0:T(8,128)} %copy.181) | copy-start | bytes 442372
  668.0 13.3 %copy-start.28 = (f32[3,3,1,64,64]{3,4,2,1,0:T(8,128)S(1)}, f32[3,3,1,64,64]{3,4,2,1,0:T(8,128)}, u32[]{:S(2)}) copy-start(f32[3,3,1,64,64]{3,4,2,1,0:T(8,128)} %copy.190) | copy-start | bytes 442372
  669.5 13.3 %copy-start.17 = (f32[3,3,4,64,64]{4,3,1,0,2:T(8,128)S(1)}, f32[3,3,4,64,64]{4,3,1,0,2:T(8,128)}, u32[]{:S(2)}) copy-start(f32[3,3,4,64,64]{4,3,1,0,2:T(8,128)} %get-tuple-element.19) | copy-start | bytes 1769476
  669.5 13.3 %copy-start.24 = (f32[3,3,64,64]{3,2,1,0:T(8,128)S(1)}, f32[3,3,64,64]{3,2,1,0:T(8,128)}, u32[]{:S(2)}) copy-start(f32[3,3,64,64]{3,2,1,0:T(8,128)} %fusion.69) | copy-start | bytes 442372
  868.9 238.2 %all-to-all-start = ((f32[16,1,204800]{2,1,0:T(1,128)}), f32[16,1,204800]{2,1,0:T(1,128)}, u32[]{:S(2)}, u32[]{:S(2)}) async-start(f32[16,1,204800]{2,1,0:T(1,128)} %reshape.348), calls=%async_computation | async-start | bytes 26214400 | tf_op jit(solution)/shard_map/all_to_all | solution.py:158
  1147.6 26.0 %copy-start.1 = (f32[4,4,4,64,64]{4,3,2,1,0:T(8,128)S(1)}, f32[4,4,4,64,64]{4,3,2,1,0:T(8,128)}, u32[]{:S(2)}) copy-start(f32[4,4,4,64,64]{4,3,2,1,0:T(8,128)} %param.10) | copy-start | bytes 3145732
  (27 other events, 214.8 us)
where the time goes:
time: 1190 us; the launch traced here: 1170 us
  waiting for transfers between devices  553 us (46%)
  matrix products  261 us (22%)
  local copies, waits for them, and re-layouts  251 us (21%)
  other arithmetic  87.1 us (7%)
  starting transfers between devices  19.4 us (2%)
    ppermute x2, waiting for transfers between devices, extended(): lax.ppermute(tail, axis, [(i, (i + 1) % count) for i in range(ends)])  323 us
    all_to_all x1, waiting for transfers between devices, body(): lax.all_to_all(outgoing, 'py', split_axis=0, concat_axis=0, tiled=True)  229 us
    dot_general x144, matrix products, galerkin_terms(): jnp.einsum('xyab,xybd->xyad', fine_rows[:, :, offset], pieces[offset][:,...  223 us
    unnamed x139, local copies, waits for them, and re-layouts  103 us
    another operation x35, local copies, waits for them, and re-layouts, galerkin_terms(): merged_list.append(jnp.stack(filled, axis=2))  56.7 us
    all_to_all x1, other arithmetic, body(): lax.all_to_all(outgoing, 'py', split_axis=0, concat_axis=0, tiled=True)  39.9 us
    concatenate x3, other arithmetic, extended(): jnp.concatenate([lax.ppermute(tail, axis, [(i, (i + 1) % count) for i in...  28 us
    dot_general x1, matrix products, galerkin_terms(): jnp.einsum('kxypba,kxynbc->xypnac', jnp.stack(own_list), jnp.stack(merged...  25.1 us
  transfers between devices with their start and end apart: 5, of which 3 were waited for; matrix products, arithmetic and copies ran while one was open for 2% of the time, Pallas kernels for 0%

commit v1 on v0

v1 whole, which is shorter than its diff:
```python
import jax
import jax.numpy as jnp
from jax import lax
from jax.experimental import pallas as pl
from jax.experimental.pallas import tpu as pltpu
from jax.sharding import PartitionSpec as P

CAP = 2
FAST_K = 6
FAST_E = 24
VM = pltpu.VMEM
SM = pltpu.SMEM
F32 = jnp.float32
BF16 = jnp.bfloat16
LIMIT = 60 * 1024 * 1024


def spec(space):
    return pl.BlockSpec(memory_space=space)


def params():
    return pltpu.CompilerParams(vmem_limit_bytes=LIMIT)


def split(value):
    high = value.astype(BF16)
    low = (value - high.astype(F32)).astype(BF16)
    return high, low


def dot3(left, right):
    out = jnp.dot(left[0], right[0], preferred_element_type=F32)
    out += jnp.dot(left[0], right[1], preferred_element_type=F32)
    out += jnp.dot(left[1], right[0], preferred_element_type=F32)
    return out


def interp_kernel(meta, cols, lens, vals, dense, west, east, south, north, corners, slots):
    coarse_y = meta[2] // 2
    slots[...] = jnp.zeros_like(slots)
    for x in range(4):
        for y in range(4):
            row_x = (meta[0] * 4 + x) // 2
            row_y = (meta[1] * 4 + y) // 2
            count = lens[x, y]
            for s in range(4):
                col = cols[x, y, s]
                place = (col % coarse_y - row_y) * 2 + (col // coarse_y - row_x)
                place = jnp.where(s < count, place, 4)
                slots[x * 4 + y, place] = vals[x, y, s]
    for x in range(4):
        for y in range(4):
            j = x * 4 + y
            block = jnp.concatenate([slots[j, q] for q in range(4)], axis=1)
            dense[j] = block
            if x == 0:
                west[y] = block
            if x == 3:
                east[y] = block
            if y == 0:
                south[x] = block
            if y == 3:
                north[x] = block
            if x in (0, 3) and y in (0, 3):
                corners[(x // 3) * 2 + y // 3] = block


def galerkin_kernel(
    meta, cols, lens, vals, dense, at_west, at_east, at_south, at_north, c00, c01, c10, c11,
    own, send, slots, phi, plo, wacc,
):
    fine_y = meta[2]
    slots[...] = jnp.zeros_like(slots)
    for x in range(4):
        for y in range(4):
            row_x = meta[0] * 4 + x
            row_y = meta[1] * 4 + y
            count = lens[x, y]
            for s in range(9):
                col = cols[x, y, s]
                place = (col // fine_y - row_x + 1) * 3 + (col % fine_y - row_y + 1)
                place = jnp.where(s < count, place, 9)
                slots[x * 4 + y, place] = vals[x, y, s]

    def interp_at(x, y):
        if 0 <= x < 4 and 0 <= y < 4:
            return dense[x * 4 + y]
        if 0 <= y < 4:
            return at_west[y] if x < 0 else at_east[y]
        if 0 <= x < 4:
            return at_south[x] if y < 0 else at_north[x]
        return {(-1, -1): c00, (-1, 4): c01, (4, -1): c10, (4, 4): c11}[(x, y)][...]

    for x in range(-1, 5):
        for y in range(-1, 5):
            n = (x + 1) * 6 + y + 1
            high, low = split(interp_at(x, y))
            phi[n] = high
            plo[n] = low
    own[...] = jnp.zeros_like(own)
    send[...] = jnp.zeros_like(send)
    for ax in range(2):
        for ay in range(2):
            wacc[...] = jnp.zeros_like(wacc)
            for dx in (-1, 0, 1):
                for dy in (-1, 0, 1):
                    lx = {-1: [0], 0: [0, 1], 1: [1]}[dx]
                    ly = {-1: [0], 0: [0, 1], 1: [1]}[dy]
                    jx = {-1: [-1], 0: [0, 1], 1: [2]}[dx]
                    jy = {-1: [-1], 0: [0, 1], 1: [2]}[dy]
                    fine_i = [(u, v) for u in lx for v in ly]
                    fine_j = [(u, v) for u in jx for v in jy]
                    left = jnp.concatenate(
                        [
                            jnp.concatenate(
                                [
                                    slots[
                                        (2 * ax + ix) * 4 + 2 * ay + iy,
                                        (u - ix + 1) * 3 + v - iy + 1,
                                    ]
                                    for u, v in fine_j
                                ],
                                axis=1,
                            )
                            for ix, iy in fine_i
                        ],
                        axis=0,
                    )
                    where = [(2 * ax + u + 1) * 6 + 2 * ay + v + 1 for u, v in fine_j]
                    right = (
                        jnp.concatenate([phi[n] for n in where], axis=0),
                        jnp.concatenate([plo[n] for n in where], axis=0),
                    )
                    product = dot3(split(left), right)
                    for n, (ix, iy) in enumerate(fine_i):
                        rows = slice((ix * 2 + iy) * 64, (ix * 2 + iy) * 64 + 64)
                        for qy in range(2):
                            at = ((dy + 1 + qy) * 4 + dx + 1) * 64
                            wacc[rows, at : at + 128] += product[
                                n * 64 : n * 64 + 64, qy * 128 : qy * 128 + 128
                            ]
            own_p = jnp.concatenate(
                [dense[(2 * ax + u) * 4 + 2 * ay + v] for u in range(2) for v in range(2)], axis=0
            )
            coarse = dot3(split(own_p.T), split(wacc[...]))
            for qy in range(2):
                for qx in range(2):
                    ix, iy = ax + qx, ay + qy
                    rows = slice((qy * 2 + qx) * 64, (qy * 2 + qx) * 64 + 64)
                    for ty in range(4):
                        piece = coarse[rows, ty * 256 : ty * 256 + 256]
                        if ix == 2:
                            at = (ty + 1 - qy) * 256
                            send[iy, :, at : at + 256] += piece
                        else:
                            at = ((ty + 1 - qy) * 5 + 1 - qx) * 64
                            own[ix * 3 + iy, :, at : at + 256] += piece


def half_tiles(piece, start, stop):
    return piece[:, start * 64 : stop * 64]


def pack_kernel(own, got, out, acc):
    for iy in range(3):
        acc[iy] = own[iy]
        for jy in range(5):
            acc[iy, :, jy * 320 : jy * 320 + 256] += got[iy, :, jy * 256 : jy * 256 + 256]
    for ix in range(2):
        row = [acc[iy] if ix == 0 else own[3 + iy] for iy in range(3)]
        for g in range(8):
            band = [r[g * 8 : g * 8 + 8] for r in row]
            out[2 * g, ix, :, 0:768] = half_tiles(band[1], 0, 12)
            out[2 * g, ix, :, 768:1536] = half_tiles(band[2], 0, 12)
            out[2 * g, ix, :, 1536:2048] = half_tiles(band[0], 4, 12)
            out[2 * g, ix, :, 2048:2176] = jnp.zeros((8, 128), F32)
            out[2 * g + 1, ix, :, 0:768] = half_tiles(band[1], 12, 24)
            out[2 * g + 1, ix, :, 768:1536] = half_tiles(band[0], 12, 24)
            out[2 * g + 1, ix, :, 1536:1664] = jnp.concatenate(
                [half_tiles(band[1], 24, 25), half_tiles(band[0], 24, 25)], axis=1
            )
            out[2 * g + 1, ix, :, 1664:2176] = half_tiles(band[2], 12, 20)


def route_kernel(kept, meta, owners, deliver, extra, source, plain, ids, need, count):
    peers = 16
    coarse_y = meta[2] // 2
    for e in range(peers):
        count[e] = 0
    for n in range(2 * peers):
        source[n] = -1
        plain[n] = -1
        ids[n] = -1

    def clear(n, carry):
        deliver[n] = 0
        return carry

    lax.fori_loop(0, peers * 32, clear, 0)

    def clear_extra(n, carry):
        extra[n] = 0
        return carry

    lax.fori_loop(0, 64, clear_extra, 0)

    def step(dy, spare):
        for k in range(4):
            e = owners[dy * 4 + k]
            rank = 0
            for before in range(k):
                rank += (owners[dy * 4 + before] == e).astype(jnp.int32)
            n = count[e]
            count[e] = n + 1
            deliver[e * 32 + n] = dy * 4 + k
            over = n >= kept
            here = jnp.where(over, kept + spare, n)
            extra[jnp.where(over, spare, 63)] = dy * 4 + k
            spare = jnp.where(over, spare + 1, spare)

            @pl.when(e == meta[1])
            def _():
                source[dy * 2 + rank] = here
                plain[dy * 2 + rank] = n
                ids[dy * 2 + rank] = (meta[0] * 2 + k // 2) * coarse_y + dy * 2 + k % 2

        return spare

    spare = lax.fori_loop(0, peers, step, 0)
    for n in range(8):
        need[n] = spare


def fan_kernel(kept, spare, meta, deliver, extra, got, *refs):
    out = refs[0]
    rows = refs[-1]
    half = meta[1] % 2

    @pl.when(half == 0)
    def _():
        def step(dy, carry):
            for ix in range(2):
                rows[dy * 4 + ix * 2, :, 0:256] = jnp.zeros((8, 256), F32)
                rows[dy * 4 + ix * 2, :, 256:768] = got[dy, ix, :, 1536:2048]
                rows[dy * 4 + ix * 2 + 1, :, 0:768] = got[dy, ix, :, 0:768]

                @pl.when(dy > 0)
                def _():
                    rows[dy * 4 + ix * 2, :, 0:768] += got[dy - 1, ix, :, 768:1536]

            return carry

        lax.fori_loop(0, 16, step, 0)

    @pl.when(half == 1)
    def _():
        def step(dy, carry):
            for ix in range(2):
                last = got[dy, ix, :, 1536:1664]
                rows[dy * 4 + ix * 2 + 1, :, 0:768] = got[dy, ix, :, 0:768]
                rows[dy * 4 + ix * 2 + 1, :, 768:896] = last
                rows[dy * 4 + ix * 2, :, 0:768] = got[dy, ix, :, 768:1536]
                rows[dy * 4 + ix * 2, :, 768:832] = last[:, 64:128]

                @pl.when(dy > 0)
                def _():
                    rows[dy * 4 + ix * 2, :, 0:512] += got[dy - 1, ix, :, 1664:2176]

            return carry

        lax.fori_loop(0, 16, step, 0)

    def place(e, carry):
        for n in range(kept):
            out[e, n] = rows[deliver[e * 32 + n]]
        return carry

    lax.fori_loop(0, 16, place, 0)
    for n in range(spare):
        refs[1][n] = rows[extra[n]]


def collect_kernel(kept, source, near, *refs):
    out = refs[-1]
    at = source[pl.program_id(0)]

    def write(get):
        for g in range(8):
            pair = (get(2 * g), get(2 * g + 1))
            for n in range(25):
                piece, lane = (pair[0], n) if n < 12 else (pair[1], n - 12)
                out[0, (n % 5) * 5 + n // 5, g * 8 : g * 8 + 8, :] = piece[
                    :, lane * 64 : lane * 64 + 64
                ]

    @pl.when(at < 0)
    def _():
        out[...] = jnp.zeros_like(out)

    @pl.when((at >= 0) & (at < kept))
    def _():
        write(lambda c: near[c, at])

    if len(refs) > 1:

        @pl.when(at >= kept)
        def _():
            write(lambda c: refs[0][c, at - kept])


def relay(kept, spare, meta, deliver, extra, source, got):
    outs = [jax.ShapeDtypeStruct((16, kept, 8, 896), F32)]
    if spare:
        outs.append(jax.ShapeDtypeStruct((spare, 8, 896), F32))
    fan = pl.pallas_call(
        lambda *refs: fan_kernel(kept, spare, *refs),
        out_shape=outs,
        in_specs=[spec(SM)] * 3 + [spec(VM)],
        out_specs=[spec(VM)] * len(outs),
        scratch_shapes=[VM((64, 8, 896), F32)],
        compiler_params=params(),
    )(meta, deliver, extra, got)
    args = []
    if spare:
        args = [lax.all_gather(fan[1], "py", axis=0, tiled=False)]
    args = [lax.all_to_all(fan[0], "py", 0, 0, tiled=True)] + args
    return pl.pallas_call(
        lambda *refs: collect_kernel(kept, *refs),
        out_shape=jax.ShapeDtypeStruct((32, 25, 64, 64), F32),
        grid_spec=pltpu.PrefetchScalarGridSpec(
            num_scalar_prefetch=1,
            grid=(32,),
            in_specs=[spec(VM)] * len(args),
            out_specs=pl.BlockSpec((1, 25, 64, 64), lambda n, source: (n, 0, 0, 0)),
        ),
        compiler_params=params(),
    )(source, *args)


def body(
    coupling_vals, coupling_cols, coupling_len, interp_vals, interp_cols, interp_len, owner_map
):
    size_x = lax.axis_size("px")
    size_y = lax.axis_size("py")
    mine_x = lax.axis_index("px")
    mine_y = lax.axis_index("py")
    meta = jnp.stack([mine_x, mine_y, 4 * size_y]).astype(jnp.int32)
    wide = jax.ShapeDtypeStruct((4, 64, 256), F32)
    dense, west, east, south, north, corners = pl.pallas_call(
        interp_kernel,
        out_shape=[jax.ShapeDtypeStruct((16, 64, 256), F32), wide, wide, wide, wide, wide],
        in_specs=[spec(SM)] * 3 + [spec(VM)],
        out_specs=[spec(VM)] * 6,
        scratch_shapes=[VM((16, 5, 64, 64), F32)],
        compiler_params=params(),
    )(meta, interp_cols, interp_len, interp_vals)

    def shift(value, dx, dy):
        pairs = [
            (x * size_y + y, (x + dx) * size_y + y + dy)
            for x in range(size_x)
            for y in range(size_y)
            if 0 <= x + dx < size_x and 0 <= y + dy < size_y
        ]
        return lax.ppermute(value, ("px", "py"), pairs)

    at_west = shift(east, 1, 0)
    at_east = shift(west, -1, 0)
    at_south = shift(north, 0, 1)
    at_north = shift(south, 0, -1)
    c00 = shift(corners[3], 1, 1)
    c01 = shift(corners[2], 1, -1)
    c10 = shift(corners[1], -1, 1)
    c11 = shift(corners[0], -1, -1)

    ints = lambda n: jax.ShapeDtypeStruct((n,), jnp.int32)
    deliver, extra, source, plain, ids, need = pl.pallas_call(
        lambda *refs: route_kernel(FAST_K, *refs),
        out_shape=[ints(16 * 32), ints(64), ints(32), ints(32), ints(32), ints(8)],
        in_specs=[spec(SM)] * 2,
        out_specs=[spec(SM)] * 6,
        scratch_shapes=[SM((16,), jnp.int32)],
    )(meta, owner_map.reshape(64))
    most = need
    for flip in (1, 2, 4):
        other = lax.ppermute(most, "px", [(x, x ^ flip) for x in range(size_x)])
        most = jnp.maximum(most, other)

    own, send = pl.pallas_call(
        galerkin_kernel,
        out_shape=[
            jax.ShapeDtypeStruct((6, 64, 1600), F32),
            jax.ShapeDtypeStruct((3, 64, 1280), F32),
        ],
        in_specs=[spec(SM)] * 3 + [spec(VM)] * 10,
        out_specs=[spec(VM)] * 2,
        scratch_shapes=[
            VM((16, 10, 64, 64), F32),
            VM((36, 64, 256), BF16),
            VM((36, 64, 256), BF16),
            VM((256, 1024), F32),
        ],
        compiler_params=params(),
    )(
        meta, coupling_cols, coupling_len, coupling_vals, dense,
        at_west, at_east, at_south, at_north, c00, c01, c10, c11,
    )
    got = shift(send, 1, 0)
    packed = pl.pallas_call(
        pack_kernel,
        out_shape=jax.ShapeDtypeStruct((16, 2, 8, 2176), F32),
        in_specs=[spec(VM)] * 2,
        out_specs=spec(VM),
        scratch_shapes=[VM((3, 64, 1600), F32)],
        compiler_params=params(),
    )(own, got)
    spread = lax.all_to_all(packed, "py", 0, 0, tiled=True)
    rows = lax.cond(
        most[0] <= FAST_E,
        lambda s: relay(FAST_K, FAST_E, meta, deliver, extra, source, s),
        lambda s: relay(32, 0, meta, deliver, extra, plain, s),
        spread,
    )
    return rows, ids


def solution(mesh):
    in_specs = (
        P("px", "py", None, None, None),
        P("px", "py", None),
        P("px", "py"),
        P("px", "py", None, None, None),
        P("px", "py", None),
        P("px", "py"),
        P("px", None, None, None),
    )
    out_specs = (P(("px", "py"), None, None, None), P(("px", "py")))
    return jax.shard_map(body, mesh=mesh, in_specs=in_specs, out_specs=out_specs, check_vma=False)
```

time: 1190 us -> 257 us (0.22)
  the two profiles are of different devices: /device:TPU:84 before, /device:TPU:13 now
where the time goes in v1:
time: 257 us; the launch traced here: 255 us
  waiting for transfers between devices  101 us (39%)
  Pallas kernels  49.9 us (19%)
  blocking collectives  48.8 us (19%)
  starting transfers between devices  36.9 us (14%)
  between operations  14.2 us (6%)
  local copies, waits for them, and re-layouts  3.54 us (1%)
    all_gather x1, waiting for transfers between devices, relay(): args = [lax.all_gather(fan[1], 'py', axis=0, tiled=False)]  57.1 us
    all_to_all x1, blocking collectives, relay(): args = [lax.all_to_all(fan[0], 'py', 0, 0, tiled=True)] + args  48.8 us
    ppermute x9, starting transfers between devices, shift(): return lax.ppermute(value, ('px', 'py'), pairs)  28.8 us
    ppermute x9, waiting for transfers between devices, shift(): return lax.ppermute(value, ('px', 'py'), pairs)  28.6 us
    pallas_call x1, Pallas kernels, relay(): pl.pallas_call(lambda *refs: collect_kernel(kept, *refs), out_shape=jax.S...  21.4 us
    pallas_call x1, Pallas kernels, body(): pl.pallas_call(galerkin_kernel, out_shape=[jax.ShapeDtypeStruct((6, 64, 1...  11.7 us
    all_to_all x1, waiting for transfers between devices, body(): spread = lax.all_to_all(packed, 'py', 0, 0, tiled=True)  9.76 us
    pallas_call x1, Pallas kernels, body(): pl.pallas_call(lambda *refs: route_kernel(FAST_K, *refs), out_shape=[ints...  5.72 us
  transfers between devices with their start and end apart: 14, of which 9 were waited for; matrix products, arithmetic and copies ran while one was open for 1% of the time, Pallas kernels for 2%

profile of v1, /device:TPU:13, one launch (start us, length us, event | category | flops | bytes accessed | tf_op | source)
XLA Modules:
  0.0 255.3 jit_solution(4734329442062124539)
XLA Ops:
  7.2 4.3 %shard_map.87 = (f32[16,64,256]{2,1,0:T(8,128)}, f32[4,64,256]{2,1,0:T(8,128)}, f32[4,64,256]{2,1,0:T(8,128)}, f32[4,64,256]{2,1,0:T(8,128)}, f32[4,64,256]{2,1,0:T(8,128)}, /*index=5*/f32[4,64,256]{2,1,0:T(8,128)}) custom-call(s32[3]{0:T(128)S(1)} %pad_add_fusion.refs_0_.meta, s32[4,4,4]{2,1,0:T(4,128)} %cols.2, s32[4,4]{1,0:T(4,128)} %lens.2, ...), custom_call_target="tpu_custom_call" | custom-call | tf_op jit(solution)/shard_map/pallas_call | solution.py:350
  12.5 6.2 %collective-permute-start.10 = (f32[64,256]{1,0:T(8,128)S(1)}, f32[64,256]{1,0:T(8,128)S(1)}, u32[]{:S(2)}, u32[]{:S(2)}) collective-permute-start(f32[64,256]{1,0:T(8,128)S(1)} %get-tuple-element.65), channel_id=1, source_target_pairs={{17,0},{18,1},{19,2},{20,3},{21,4},{22,5},{23,6},{24,7},{25,8},{26... | collective-permute-start | bytes 196616 | tf_op jit(solution)/shard_map/ppermute | solution.py:366
  18.7 2.8 %collective-permute-start.3 = (f32[4,64,256]{2,1,0:T(8,128)}, f32[4,64,256]{2,1,0:T(8,128)S(1)}, u32[]{:S(2)}, u32[]{:S(2)}) collective-permute-start(f32[4,64,256]{2,1,0:T(8,128)} %get-tuple-element.55), channel_id=1, source_target_pairs={{0,16},{1,17},{2,18},{3,19},{4,20},{5,21},{6,22},{7,23},{8,24},{9,... | collective-permute-start | bytes 786440 | tf_op jit(solution)/shard_map/ppermute | solution.py:366
  25.4 5.5 %collective-permute-start.6 = (f32[4,64,256]{2,1,0:T(8,128)}, f32[4,64,256]{2,1,0:T(8,128)S(1)}, u32[]{:S(2)}, u32[]{:S(2)}) collective-permute-start(f32[4,64,256]{2,1,0:T(8,128)} %get-tuple-element.58), channel_id=1, source_target_pairs={{1,0},{2,1},{3,2},{4,3},{5,4},{6,5},{7,6},{8,7},{9,8},{10,9},{11,1... | collective-permute-start | bytes 786440 | tf_op jit(solution)/shard_map/ppermute | solution.py:366
  30.9 1.9 collective-permute-start.9
  32.8 7.1 %collective-permute-done.9.c10 = f32[64,256]{1,0:T(8,128)S(1)} collective-permute-done((f32[64,256]{1,0:T(8,128)S(1)}, f32[64,256]{1,0:T(8,128)S(1)}, u32[]{:S(2)}, u32[]{:S(2)}) %collective-permute-start.9) | collective-permute-done | bytes 65568 | tf_op jit(solution)/shard_map/ppermute | solution.py:366
  41.8 4.5 %collective-permute-done.8.c01 = f32[64,256]{1,0:T(8,128)S(1)} collective-permute-done((f32[64,256]{1,0:T(8,128)S(1)}, f32[64,256]{1,0:T(8,128)S(1)}, u32[]{:S(2)}, u32[]{:S(2)}) %collective-permute-start.8) | collective-permute-done | bytes 65568 | tf_op jit(solution)/shard_map/ppermute | solution.py:366
  46.3 2.0 collective-permute-start.7
  48.3 5.7 %collective-permute-done.7.c00 = f32[64,256]{1,0:T(8,128)S(1)} collective-permute-done((f32[64,256]{1,0:T(8,128)S(1)}, f32[64,256]{1,0:T(8,128)S(1)}, u32[]{:S(2)}, u32[]{:S(2)}) %collective-permute-start.7) | collective-permute-done | bytes 65568 | tf_op jit(solution)/shard_map/ppermute | solution.py:366
  55.0 11.7 %shard_map.88 = (f32[6,64,1600]{2,1,0:T(8,128)}, f32[3,64,1280]{2,1,0:T(8,128)}) custom-call(s32[3]{0:T(128)S(1)} %pad_add_fusion.refs_0_.meta, s32[4,4,9]{2,1,0:T(4,128)} %cols.3, s32[4,4]{1,0:T(4,128)} %lens.3, f32[4,4,9,64,64]{4,3,2,1,0:T(8,128)} %vals.3, f32[16,64,256]{2,1,0:T(8,128)} %get-tuple-element.54.dense, f32[4,64,256]{2,1,0:T(8,128)} %copy-done.1, ...), custom_call_target="tpu_custom_call" | custom-call | tf_op jit(solution)/shard_map/pallas_call | solution.py:390
  66.7 4.7 %collective-permute-start.11 = (f32[3,64,1280]{2,1,0:T(8,128)}, f32[3,64,1280]{2,1,0:T(8,128)S(1)}, u32[]{:S(2)}, u32[]{:S(2)}) collective-permute-start(f32[3,64,1280]{2,1,0:T(8,128)} %get-tuple-element.61), channel_id=1, source_target_pairs={{0,16},{1,17},{2,18},{3,19},{4,20},{5,21},{6,22},{7,23},{8,24},{9,... | collective-permute-start | bytes 2949128 | tf_op jit(solution)/shard_map/ppermute | solution.py:366
  71.4 11.3 %collective-permute-done.11.got = f32[3,64,1280]{2,1,0:T(8,128)S(1)} collective-permute-done((f32[3,64,1280]{2,1,0:T(8,128)}, f32[3,64,1280]{2,1,0:T(8,128)S(1)}, u32[]{:S(2)}, u32[]{:S(2)}) %collective-permute-start.11) | collective-permute-done | bytes 983072 | tf_op jit(solution)/shard_map/ppermute | solution.py:366
  83.7 3.7 %shard_map.89 = f32[16,2,8,2176]{3,2,1,0:T(8,128)} custom-call(f32[6,64,1600]{2,1,0:T(8,128)} %get-tuple-element.60.own, f32[3,64,1280]{2,1,0:T(8,128)} %copy-done), custom_call_target="tpu_custom_call" | custom-call | tf_op jit(solution)/shard_map/pallas_call | solution.py:410
  87.4 4.3 %all-to-all-start.2 = ((f32[16,2,8,2176]{3,2,1,0:T(8,128)}), f32[16,2,8,2176]{3,2,1,0:T(8,128)S(1)}, u32[]{:S(2)}, u32[]{:S(2)}) async-start(f32[16,2,8,2176]{3,2,1,0:T(8,128)} %shard_map.89), calls=%async_computation.2 | async-start | bytes 4456448 | tf_op jit(solution)/shard_map/all_to_all | solution.py:418
  92.3 5.7 %shard_map.86 = (s32[512]{0:T(512)S(1)}, s32[64]{0:T(128)S(1)}, s32[32]{0:T(128)S(1)}, s32[32]{0:T(128)S(1)}, s32[32]{0:T(128)}, /*index=5*/s32[8]{0:T(128)}) custom-call(s32[3]{0:T(128)S(1)} %pad_add_fusion.refs_0_.meta, s32[64]{0:T(128)} %reshape.11.refs_1_), custom_call_target="tpu_custom_call" | custom-call | tf_op jit(solution)/shard_map/pallas_call | solution.py:378
  101.4 2.7 %collective-permute-done.1 = s32[8]{0:T(128)S(1)} collective-permute-done((s32[8]{0:T(128)S(1)}, s32[8]{0:T(128)S(1)}, u32[]{:S(2)}, u32[]{:S(2)}) %collective-permute-start.1) | collective-permute-done | bytes 64 | tf_op jit(solution)/shard_map/ppermute | solution.py:387
  104.0 2.2 collective-permute-start.2
  106.2 2.0 collective-permute-done.2
  108.3 9.8 %all-to-all-done.2 = f32[16,2,8,2176]{3,2,1,0:T(8,128)S(1)} async-done(((f32[16,2,8,2176]{3,2,1,0:T(8,128)}), f32[16,2,8,2176]{3,2,1,0:T(8,128)S(1)}, u32[]{:S(2)}, u32[]{:S(2)}) %all-to-all-start.2) | async-done | bytes 2228256 | tf_op jit(solution)/shard_map/all_to_all | solution.py:418
  118.0 130.5 %conditional.1 = (f32[32,25,64,64]{3,2,1,0:T(8,128)}) conditional(s32[]{:T(128)} %bitcast.3, (s32[3]{0:T(128)S(1)}, s32[512]{0:T(512)S(1)}, s32[64]{0:T(128)S(1)}, f32[16,2,8,2176]{3,2,1,0:T(8,128)S(1)}, s32[32]{0:T(128)S(1)}) %tuple.14, (s32[3]{0:T(128)S(1)}, s32[512]{0:T(512)S(1)}, s32[64]{0:T(128)S(1)}, f32[16,2,8,2176]{3,2,1,0:T(8,128)S(1)}, ...), branch_computations={%region_0.0_spmd, %region_1.0_spmd} | conditional | bytes 40599600 | solution.py:419
  118.1 3.0 %branch_1_fun.2 = (f32[16,6,8,896]{3,2,1,0:T(8,128)}, f32[24,8,896]{2,1,0:T(8,128)}) custom-call(s32[3]{0:T(128)S(1)} %get-tuple-element.29.refs_0_, s32[512]{0:T(512)S(1)} %get-tuple-element.30.refs_1_, s32[64]{0:T(128)S(1)} %get-tuple-element.31.refs_2_, f32[16,2,8,2176]{3,2,1,0:T(8,128)S(1)} %get-tuple-element.32.refs_3_), custom_call_target="tpu_custom_call" | custom-call | tf_op jit(solution)/shard_map/cond/branch_1_fun/pallas_call | solution.py:316
  121.1 48.8 %all_to_all.14.refs_1_ = f32[16,6,8,896]{3,2,1,0:T(8,128)} all-to-all(f32[16,6,8,896]{3,2,1,0:T(8,128)} %get-tuple-element.33), channel_id=1, replica_groups=mesh['px'=8,'py'=16] {'py'}, dimensions={0} | all-to-all | bytes 5505024 | tf_op jit(solution)/shard_map/cond/branch_1_fun/all_to_all | solution.py:327
  169.9 57.1 %all-gather.3.cloned.1.call-done = f32[384,8,896]{2,1,0:T(8,128)} async-done(((f32[24,8,896]{2,1,0:T(8,128)}), f32[384,8,896]{2,1,0:T(8,128)}) %all-gather.3.cloned.1.call-update) | async-done | bytes 11010064 | tf_op jit(solution)/shard_map/cond/branch_1_fun/all_gather | solution.py:326
  227.1 21.4 %branch_1_fun.3 = f32[32,25,64,64]{3,2,1,0:T(8,128)} custom-call(s32[32]{0:T(128)S(1)} %get-tuple-element.28.refs_0_, f32[16,6,8,896]{3,2,1,0:T(8,128)} %all_to_all.14.refs_1_, f32[16,24,8,896]{3,2,1,0:T(8,128)} %bitcast.17), custom_call_target="tpu_custom_call" | custom-call | tf_op jit(solution)/shard_map/cond/branch_1_fun/pallas_call | solution.py:328
  (40 shorter events, 12.7 us)
Async XLA Ops:
  12.5 18.4 %collective-permute-start.10 = (f32[64,256]{1,0:T(8,128)S(1)}, f32[64,256]{1,0:T(8,128)S(1)}, u32[]{:S(2)}, u32[]{:S(2)}) collective-permute-start(f32[64,256]{1,0:T(8,128)S(1)} %get-tuple-element.65), channel_id=1, source_target_pairs={{17,0},{18,1},{19,2},{20,3},{21,4},{22,5},{23,6},{24,7},{25,8},{26... | collective-permute-start | bytes 196616 | tf_op jit(solution)/shard_map/ppermute | solution.py:366
  18.7 35.3 %collective-permute-start.3 = (f32[4,64,256]{2,1,0:T(8,128)}, f32[4,64,256]{2,1,0:T(8,128)S(1)}, u32[]{:S(2)}, u32[]{:S(2)}) collective-permute-start(f32[4,64,256]{2,1,0:T(8,128)} %get-tuple-element.55), channel_id=1, source_target_pairs={{0,16},{1,17},{2,18},{3,19},{4,20},{5,21},{6,22},{7,23},{8,24},{9,... | collective-permute-start | bytes 786440 | tf_op jit(solution)/shard_map/ppermute | solution.py:366
  21.5 32.5 %collective-permute-start.4 = (f32[4,64,256]{2,1,0:T(8,128)}, f32[4,64,256]{2,1,0:T(8,128)S(1)}, u32[]{:S(2)}, u32[]{:S(2)}) collective-permute-start(f32[4,64,256]{2,1,0:T(8,128)} %get-tuple-element.56), channel_id=1, source_target_pairs={{16,0},{17,1},{18,2},{19,3},{20,4},{21,5},{22,6},{23,7},{24,8},{25... | collective-permute-start | bytes 786440 | tf_op jit(solution)/shard_map/ppermute | solution.py:366
  23.4 30.6 %collective-permute-start.5 = (f32[4,64,256]{2,1,0:T(8,128)}, f32[4,64,256]{2,1,0:T(8,128)S(1)}, u32[]{:S(2)}, u32[]{:S(2)}) collective-permute-start(f32[4,64,256]{2,1,0:T(8,128)} %get-tuple-element.57), channel_id=1, source_target_pairs={{0,1},{1,2},{2,3},{3,4},{4,5},{5,6},{6,7},{7,8},{8,9},{9,10},{10,1... | collective-permute-start | bytes 786440 | tf_op jit(solution)/shard_map/ppermute | solution.py:366
  25.4 28.7 %collective-permute-start.6 = (f32[4,64,256]{2,1,0:T(8,128)}, f32[4,64,256]{2,1,0:T(8,128)S(1)}, u32[]{:S(2)}, u32[]{:S(2)}) collective-permute-start(f32[4,64,256]{2,1,0:T(8,128)} %get-tuple-element.58), channel_id=1, source_target_pairs={{1,0},{2,1},{3,2},{4,3},{5,4},{6,5},{7,6},{8,7},{9,8},{10,9},{11,1... | collective-permute-start | bytes 786440 | tf_op jit(solution)/shard_map/ppermute | solution.py:366
  30.9 23.2 %copy-start.5 = (f32[64,256]{1,0:T(8,128)}, f32[64,256]{1,0:T(8,128)S(1)}, u32[]{:S(2)}) copy-start(f32[64,256]{1,0:T(8,128)S(1)} %collective-permute-done.10.c11) | copy-start | bytes 196612
  30.9 9.0 %collective-permute-start.9 = (f32[64,256]{1,0:T(8,128)S(1)}, f32[64,256]{1,0:T(8,128)S(1)}, u32[]{:S(2)}, u32[]{:S(2)}) collective-permute-start(f32[64,256]{1,0:T(8,128)S(1)} %get-tuple-element.66), channel_id=1, source_target_pairs={{16,1},{17,2},{18,3},{19,4},{20,5},{21,6},{22,7},{23,8},{24,9},{25... | collective-permute-start | bytes 196616 | tf_op jit(solution)/shard_map/ppermute | solution.py:366
  39.9 14.2 %copy-start.6 = (f32[64,256]{1,0:T(8,128)}, f32[64,256]{1,0:T(8,128)S(1)}, u32[]{:S(2)}) copy-start(f32[64,256]{1,0:T(8,128)S(1)} %collective-permute-done.9.c10) | copy-start | bytes 196612
  39.9 6.5 %collective-permute-start.8 = (f32[64,256]{1,0:T(8,128)S(1)}, f32[64,256]{1,0:T(8,128)S(1)}, u32[]{:S(2)}, u32[]{:S(2)}) collective-permute-start(f32[64,256]{1,0:T(8,128)S(1)} %get-tuple-element.67), channel_id=1, source_target_pairs={{1,16},{2,17},{3,18},{4,19},{5,20},{6,21},{7,22},{8,23},{9,24},{10... | collective-permute-start | bytes 196616 | tf_op jit(solution)/shard_map/ppermute | solution.py:366
  46.3 7.8 %copy-start.7 = (f32[64,256]{1,0:T(8,128)}, f32[64,256]{1,0:T(8,128)S(1)}, u32[]{:S(2)}) copy-start(f32[64,256]{1,0:T(8,128)S(1)} %collective-permute-done.8.c01) | copy-start | bytes 196612
  46.3 7.7 %collective-permute-start.7 = (f32[64,256]{1,0:T(8,128)S(1)}, f32[64,256]{1,0:T(8,128)S(1)}, u32[]{:S(2)}, u32[]{:S(2)}) collective-permute-start(f32[64,256]{1,0:T(8,128)S(1)} %get-tuple-element.68), channel_id=1, source_target_pairs={{0,17},{1,18},{2,19},{3,20},{4,21},{5,22},{6,23},{7,24},{8,25},{9,... | collective-permute-start | bytes 196616 | tf_op jit(solution)/shard_map/ppermute | solution.py:366
  54.0 0.6 copy-start.8
  54.0 0.7 copy-start.1
  54.0 0.8 copy-start.2
  54.0 0.9 copy-start.3
  54.1 1.0 copy-start.4
  66.7 16.0 %collective-permute-start.11 = (f32[3,64,1280]{2,1,0:T(8,128)}, f32[3,64,1280]{2,1,0:T(8,128)S(1)}, u32[]{:S(2)}, u32[]{:S(2)}) collective-permute-start(f32[3,64,1280]{2,1,0:T(8,128)} %get-tuple-element.61), channel_id=1, source_target_pairs={{0,16},{1,17},{2,18},{3,19},{4,20},{5,21},{6,22},{7,23},{8,24},{9,... | collective-permute-start | bytes 2949128 | tf_op jit(solution)/shard_map/ppermute | solution.py:366
  82.7 1.0 copy-start
  83.7 8.0 %copy-start.9 = (s32[1,16,4,1]{1,3,2,0:T(1,128)S(1)}, s32[1,16,4,1]{1,3,2,0:T(1,128)}, u32[]{:S(2)}) copy-start(s32[1,16,4,1]{1,3,2,0:T(1,128)} %param.15) | copy-start | bytes 772
  87.4 30.7 %all-to-all-start.2 = ((f32[16,2,8,2176]{3,2,1,0:T(8,128)}), f32[16,2,8,2176]{3,2,1,0:T(8,128)S(1)}, u32[]{:S(2)}, u32[]{:S(2)}) async-start(f32[16,2,8,2176]{3,2,1,0:T(8,128)} %shard_map.89), calls=%async_computation.2 | async-start | bytes 4456448 | tf_op jit(solution)/shard_map/all_to_all | solution.py:418
  98.1 2.7 %collective-permute-start = (s32[8]{0:T(128)}, s32[8]{0:T(128)S(1)}, u32[]{:S(2)}, u32[]{:S(2)}) collective-permute-start(s32[8]{0:T(128)} %get-tuple-element.51), channel_id=1, source_target_pairs={{0,16},{16,0},{32,48},{48,32},{64,80},{80,64},{96,112},{112,96},{1... | collective-permute-start | bytes 104 | tf_op jit(solution)/shard_map/ppermute | solution.py:387
  101.4 2.7 %collective-permute-start.1 = (s32[8]{0:T(128)S(1)}, s32[8]{0:T(128)S(1)}, u32[]{:S(2)}, u32[]{:S(2)}) collective-permute-start(s32[8]{0:T(128)S(1)} %max.9), channel_id=1, source_target_pairs={{0,32},{16,48},{32,0},{48,16},{64,96},{80,112},{96,64},{112,80},{1... | collective-permute-start | bytes 104 | tf_op jit(solution)/shard_map/ppermute | solution.py:387
  104.0 4.2 %collective-permute-start.2 = (s32[8]{0:T(128)S(1)}, s32[8]{0:T(128)S(1)}, u32[]{:S(2)}, u32[]{:S(2)}) collective-permute-start(s32[8]{0:T(128)S(1)} %max.10), channel_id=1, source_target_pairs={{0,64},{16,80},{32,96},{48,112},{64,0},{80,16},{96,32},{112,48},{1... | collective-permute-start | bytes 104 | tf_op jit(solution)/shard_map/ppermute | solution.py:387
  118.0 109.0 %all-gather.3.cloned.1.call-start = ((), (), s32[]{:S(2)}) async-start(), calls=%async_computation.3 | async-start | bytes 11698176 | tf_op jit(solution)/shard_map/cond/branch_1_fun/all_gather | solution.py:326
Sparse Core Ops, SparseCore 0:
  121.2 105.7 all-gather.2

commit v2 on v1

v2 whole, which is shorter than its diff:
```python
import jax
import jax.numpy as jnp
from jax import lax
from jax.experimental import pallas as pl
from jax.experimental.pallas import tpu as pltpu
from jax.sharding import PartitionSpec as P

KEPT = 6
SPARES = (14, 16, 18, 22)
BUFFERS = 4
VM = pltpu.VMEM
SM = pltpu.SMEM
F32 = jnp.float32
BF16 = jnp.bfloat16
LIMIT = 60 * 1024 * 1024


def spec(space):
    return pl.BlockSpec(memory_space=space)


def params():
    return pltpu.CompilerParams(vmem_limit_bytes=LIMIT)


def split(value):
    high = value.astype(BF16)
    low = (value - high.astype(F32)).astype(BF16)
    return high, low


def dot3(left, right):
    out = jnp.dot(left[0], right[0], preferred_element_type=F32)
    out += jnp.dot(left[0], right[1], preferred_element_type=F32)
    out += jnp.dot(left[1], right[0], preferred_element_type=F32)
    return out


def interp_kernel(meta, cols, lens, vals, dense, south, north, slots):
    coarse_y = meta[2] // 2
    slots[...] = jnp.zeros_like(slots)
    for x in range(4):
        for y in range(4):
            row_x = (meta[0] * 4 + x) // 2
            row_y = (meta[1] * 4 + y) // 2
            count = lens[x, y]
            for s in range(4):
                col = cols[x, y, s]
                place = (col % coarse_y - row_y) * 2 + (col // coarse_y - row_x)
                place = jnp.where(s < count, place, 4)
                slots[x * 4 + y, place] = vals[x, y, s]
    for x in range(4):
        for y in range(4):
            j = x * 4 + y
            block = jnp.concatenate([slots[j, q] for q in range(4)], axis=1)
            dense[j] = block
            if y == 0:
                south[x] = block
            if y == 3:
                north[x] = block


NEAR = {-1: [0], 0: [0, 1], 1: [1]}
FAR = {-1: [-1], 0: [0, 1], 1: [2]}


def sheet(dx, dy):
    if dx == 0 and dy == 0:
        return slice(0, 256), slice(0, 256)
    if dy == 0:
        return (slice(0, 128) if dx < 0 else slice(128, 256)), slice(256, 384)
    if dx == 0:
        return (slice(0, 128) if dy < 0 else slice(128, 256)), slice(384, 512)
    at = ((dx > 0) * 2 + (dy > 0)) * 64
    return slice(at, at + 64), slice(512, 576)


def prepare_kernel(meta, cols, lens, vals, dense, left, turned, slots):
    fine_y = meta[2]
    slots[...] = jnp.zeros_like(slots)
    for x in range(4):
        for y in range(4):
            row_x = meta[0] * 4 + x
            row_y = meta[1] * 4 + y
            count = lens[x, y]
            for s in range(9):
                col = cols[x, y, s]
                place = (col // fine_y - row_x + 1) * 3 + (col % fine_y - row_y + 1)
                place = jnp.where(s < count, place, 9)
                slots[x * 4 + y, place] = vals[x, y, s]
    for ax in range(2):
        for ay in range(2):
            for dx in (-1, 0, 1):
                for dy in (-1, 0, 1):
                    fine_i = [(u, v) for u in NEAR[dx] for v in NEAR[dy]]
                    fine_j = [(u, v) for u in FAR[dx] for v in FAR[dy]]
                    rows, columns = sheet(dx, dy)
                    for n, (ix, iy) in enumerate(fine_i):
                        band = jnp.concatenate(
                            [
                                slots[
                                    (2 * ax + ix) * 4 + 2 * ay + iy,
                                    (u - ix + 1) * 3 + v - iy + 1,
                                ]
                                for u, v in fine_j
                            ],
                            axis=1,
                        )
                        at = slice(rows.start + n * 64, rows.start + n * 64 + 64)
                        high, low = split(band)
                        left[ax, ay, 0, at, columns] = high
                        left[ax, ay, 1, at, columns] = low
            own_p = jnp.concatenate(
                [dense[(2 * ax + u) * 4 + 2 * ay + v] for u in range(2) for v in range(2)], axis=0
            )
            high, low = split(own_p.T)
            turned[ax, ay, 0] = high
            turned[ax, ay, 1] = low


def galerkin_kernel(ax, left, turned, dense, side, at_south, at_north, *refs):
    phi, plo, wacc = refs[-3:]
    for x in range(4):
        for y in range(6):
            at_x, at_y = 2 * ax - 1 + x, y - 1
            if at_x < 0 or at_x > 3:
                block = side[y]
            elif at_y < 0:
                block = at_south[at_x]
            elif at_y > 3:
                block = at_north[at_x]
            else:
                block = dense[at_x * 4 + at_y]
            high, low = split(block)
            phi[x * 6 + y] = high
            plo[x * 6 + y] = low

    if ax == 1:
        send, part = refs[:2]
        send[...] = jnp.zeros_like(send)
        part[...] = jnp.zeros_like(part)
    else:
        part, own, out, acc = refs[:4]
        own[...] = jnp.zeros_like(own)
        acc[...] = part[...]

    for ay in range(2):
        wacc[...] = jnp.zeros_like(wacc)
        for dx in (-1, 0, 1):
            for dy in (-1, 0, 1):
                fine_i = [(u, v) for u in NEAR[dx] for v in NEAR[dy]]
                fine_j = [(u, v) for u in FAR[dx] for v in FAR[dy]]
                rows, columns = sheet(dx, dy)
                where = [(u + 1) * 6 + 2 * ay + v + 1 for u, v in fine_j]
                right = (
                    jnp.concatenate([phi[n] for n in where], axis=0),
                    jnp.concatenate([plo[n] for n in where], axis=0),
                )
                product = dot3(
                    (left[0, ay, 0, rows, columns], left[0, ay, 1, rows, columns]), right
                )
                for n, (ix, iy) in enumerate(fine_i):
                    at_row = slice((ix * 2 + iy) * 64, (ix * 2 + iy) * 64 + 64)
                    for qy in range(2):
                        at = ((dy + 1 + qy) * 4 + dx + 1) * 64
                        wacc[at_row, at : at + 128] += product[
                            n * 64 : n * 64 + 64, qy * 128 : qy * 128 + 128
                        ]
        coarse = dot3((turned[0, ay, 0], turned[0, ay, 1]), split(wacc[...]))
        for qy in range(2):
            for qx in range(2):
                rows = slice((qy * 2 + qx) * 64, (qy * 2 + qx) * 64 + 64)
                for ty in range(4):
                    piece = coarse[rows, ty * 256 : ty * 256 + 256]
                    at = ((ty + 1 - qy) * 5 + 1 - qx) * 64
                    if ax == 1 and qx == 1:
                        at = (ty + 1 - qy) * 256
                        send[ay + qy, :, at : at + 256] += piece
                    elif ax == 1:
                        part[ay + qy, :, at : at + 256] += piece
                    elif qx == 1:
                        acc[ay + qy, :, at : at + 256] += piece
                    else:
                        own[ay + qy, :, at : at + 256] += piece
    if ax == 0:
        pack_rows([acc[iy] for iy in range(3)], out, 1)


def half_tiles(piece, start, stop):
    return piece[:, start * 64 : stop * 64]


def pack_rows(row, out, ix):
    for g in range(8):
        band = [r[g * 8 : g * 8 + 8] for r in row]
        out[2 * g, ix, :, 0:768] = half_tiles(band[1], 0, 12)
        out[2 * g, ix, :, 768:1536] = half_tiles(band[2], 0, 12)
        out[2 * g, ix, :, 1536:2048] = half_tiles(band[0], 4, 12)
        out[2 * g, ix, :, 2048:2176] = jnp.zeros((8, 128), F32)
        out[2 * g + 1, ix, :, 0:768] = half_tiles(band[1], 12, 24)
        out[2 * g + 1, ix, :, 768:1536] = half_tiles(band[0], 12, 24)
        out[2 * g + 1, ix, :, 1536:1664] = jnp.concatenate(
            [half_tiles(band[1], 24, 25), half_tiles(band[0], 24, 25)], axis=1
        )
        out[2 * g + 1, ix, :, 1664:2176] = half_tiles(band[2], 12, 20)


def pack_kernel(own, got, packed, out, acc):
    for iy in range(3):
        acc[iy] = own[iy]
        for jy in range(5):
            acc[iy, :, jy * 320 : jy * 320 + 256] += got[iy, :, jy * 256 : jy * 256 + 256]
    pack_rows([acc[iy] for iy in range(3)], out, 0)


def route_kernel(meta, owners, deliver, extra, source, plain, ids, pick, count):
    peers = 16
    coarse_y = meta[2] // 2
    for e in range(peers):
        count[e] = 0
    for n in range(2 * peers):
        source[n] = -1
        plain[n] = -1
        ids[n] = -1

    def clear(n, carry):
        for m in range(8):
            deliver[n * 8 + m] = 0
        return carry

    lax.fori_loop(0, peers * 32 // 8, clear, 0)
    for n in range(64):
        extra[n] = 0

    def step(dy, spare):
        for k in range(4):
            e = owners[dy * 4 + k]
            rank = 0
            for before in range(k):
                rank += (owners[dy * 4 + before] == e).astype(jnp.int32)
            n = count[e]
            count[e] = n + 1
            deliver[e * 32 + n] = dy * 4 + k
            over = n >= KEPT
            here = jnp.where(over, KEPT + spare, n)
            extra[jnp.where(over, spare, 63)] = dy * 4 + k
            spare = jnp.where(over, spare + 1, spare)

            @pl.when(e == meta[1])
            def _():
                source[dy * 2 + rank] = here
                plain[dy * 2 + rank] = n
                ids[dy * 2 + rank] = (meta[0] * 2 + k // 2) * coarse_y + dy * 2 + k % 2

        return spare

    spare = lax.fori_loop(0, peers, step, 0)
    branch = 0
    for most in SPARES:
        branch += (spare > most).astype(jnp.int32)
    for n in range(8):
        pick[n] = branch


def put_pair(out, first, second):
    out[:, 0:768] = first[:, 0:768]
    out[:, 768:1536] = second[:, 0:768]
    out[:, 1536:1664] = jnp.concatenate([first[:, 768:832], second[:, 768:832]], axis=1)


def fan_kernel(kept, spare, meta, deliver, extra, got, *refs):
    rows = refs[-1]
    half = meta[1] % 2

    @pl.when(half == 0)
    def _():
        def step(dy, carry):
            for ix in range(2):
                rows[dy * 4 + ix * 2, :, 0:256] = jnp.zeros((8, 256), F32)
                rows[dy * 4 + ix * 2, :, 256:768] = got[dy, ix, :, 1536:2048]
                rows[dy * 4 + ix * 2 + 1, :, 0:768] = got[dy, ix, :, 0:768]

                @pl.when(dy > 0)
                def _():
                    rows[dy * 4 + ix * 2, :, 0:768] += got[dy - 1, ix, :, 768:1536]

            return carry

        lax.fori_loop(0, 16, step, 0)

    @pl.when(half == 1)
    def _():
        def step(dy, carry):
            for ix in range(2):
                last = got[dy, ix, :, 1536:1664]
                rows[dy * 4 + ix * 2 + 1, :, 0:768] = got[dy, ix, :, 0:768]
                rows[dy * 4 + ix * 2 + 1, :, 768:896] = last
                rows[dy * 4 + ix * 2, :, 0:768] = got[dy, ix, :, 768:1536]
                rows[dy * 4 + ix * 2, :, 768:832] = last[:, 64:128]

                @pl.when(dy > 0)
                def _():
                    rows[dy * 4 + ix * 2, :, 0:512] += got[dy - 1, ix, :, 1664:2176]

            return carry

        lax.fori_loop(0, 16, step, 0)

    def place(e, carry):
        for n in range(kept // 2):
            at = e * 32 + 2 * n
            put_pair(refs[0].at[e, n], rows[deliver[at]], rows[deliver[at + 1]])
        return carry

    lax.fori_loop(0, 16, place, 0)
    for n in range(spare // 2):
        put_pair(refs[1].at[n], rows[extra[2 * n]], rows[extra[2 * n + 1]])


def collect_kernel(low, high, first, source, parts, *refs):
    out, built, blank, sems = refs[-4:]

    def build(slot, at):
        pair = at // 2
        odd = at % 2
        start = pl.multiple_of(odd * 768, 128)
        for g in range(8):
            left = parts[2 * g, pair, :, pl.ds(start, 768)]
            right = parts[2 * g + 1, pair, :, pl.ds(start, 768)]
            last = parts[2 * g + 1, pair, :, 1536:1664]
            last = jnp.where(odd == 0, last[:, 0:64], last[:, 64:128])
            for n in range(25):
                if n < 12:
                    piece = left[:, n * 64 : n * 64 + 64]
                elif n < 24:
                    piece = right[:, (n - 12) * 64 : (n - 12) * 64 + 64]
                else:
                    piece = last
                built[slot, (n % 5) * 5 + n // 5, g * 8 : g * 8 + 8, :] = piece

    def wait(buffer):
        pltpu.make_async_copy(built.at[buffer], out.at[0], sems.at[buffer]).wait()

    if first:
        blank[...] = jnp.zeros_like(blank)

        def clear(slot, carry):
            @pl.when(source[slot] < 0)
            def _():
                pltpu.make_async_copy(blank, out.at[slot], sems.at[BUFFERS]).start()

            return carry

        lax.fori_loop(0, 32, clear, 0)

    def step(slot, done):
        at = source[slot]
        here = (at >= low) & (at < high)
        buffer = done % BUFFERS

        @pl.when(here & (done >= BUFFERS))
        def _():
            wait(buffer)

        @pl.when(here)
        def _():
            build(buffer, at - low)
            pltpu.make_async_copy(built.at[buffer], out.at[slot], sems.at[buffer]).start()

        return jnp.where(here, done + 1, done)

    done = lax.fori_loop(0, 32, step, 0)
    for buffer in range(BUFFERS):

        @pl.when(done > buffer)
        def _():
            wait(buffer)

    if first:

        def settle(slot, carry):
            @pl.when(source[slot] < 0)
            def _():
                pltpu.make_async_copy(blank, out.at[0], sems.at[BUFFERS]).wait()

            return carry

        lax.fori_loop(0, 32, settle, 0)


def collect(low, high, source, parts, base=None):
    args = [source, parts] + ([] if base is None else [base])
    return pl.pallas_call(
        lambda *refs: collect_kernel(low, high, base is None, *refs),
        out_shape=jax.ShapeDtypeStruct((32, 25, 64, 64), F32),
        in_specs=[spec(SM), spec(VM), spec(pl.ANY)][: len(args)],
        out_specs=spec(pl.ANY),
        scratch_shapes=[
            VM((BUFFERS, 25, 64, 64), F32),
            VM((25, 64, 64), F32),
            pltpu.SemaphoreType.DMA((BUFFERS + 1,)),
        ],
        input_output_aliases={} if base is None else {2: 0},
        compiler_params=params(),
    )(*args)


def relay(kept, spare, meta, deliver, extra, source, got):
    outs = [jax.ShapeDtypeStruct((16, kept // 2, 8, 1664), F32)]
    if spare:
        outs.append(jax.ShapeDtypeStruct((spare // 2, 8, 1664), F32))
    fan = pl.pallas_call(
        lambda *refs: fan_kernel(kept, spare, *refs),
        out_shape=outs,
        in_specs=[spec(SM)] * 3 + [spec(VM)],
        out_specs=[spec(VM)] * len(outs),
        scratch_shapes=[VM((64, 8, 896), F32)],
        compiler_params=params(),
    )(meta, deliver, extra, got)
    if spare:
        far = lax.all_gather(fan[1], "py", axis=0, tiled=False)
    near = lax.all_to_all(fan[0], "py", 0, 0, tiled=True)
    rows = collect(0, kept, source, near)
    if spare:
        rows = collect(kept, kept + spare, source, far, rows)
    return rows


def body(
    coupling_vals, coupling_cols, coupling_len, interp_vals, interp_cols, interp_len, owner_map
):
    size_x = lax.axis_size("px")
    size_y = lax.axis_size("py")
    mine_x = lax.axis_index("px")
    mine_y = lax.axis_index("py")
    meta = jnp.stack([mine_x, mine_y, 4 * size_y]).astype(jnp.int32)
    edge = jax.ShapeDtypeStruct((4, 64, 256), F32)
    dense, south, north = pl.pallas_call(
        interp_kernel,
        out_shape=[jax.ShapeDtypeStruct((16, 64, 256), F32), edge, edge],
        in_specs=[spec(SM)] * 3 + [spec(VM)],
        out_specs=[spec(VM)] * 3,
        scratch_shapes=[VM((16, 5, 64, 64), F32)],
        compiler_params=params(),
    )(meta, interp_cols, interp_len, interp_vals)

    def shift(value, axis, step):
        count = lax.axis_size(axis)
        pairs = [(i, i + step) for i in range(count) if 0 <= i + step < count]
        return lax.ppermute(value, axis, pairs)

    at_south = shift(north, "py", 1)
    at_north = shift(south, "py", -1)
    west = jnp.concatenate([at_south[:1], dense[:4], at_north[:1]], axis=0)
    east = jnp.concatenate([at_south[3:], dense[12:], at_north[3:]], axis=0)
    left, turned = pl.pallas_call(
        prepare_kernel,
        out_shape=[
            jax.ShapeDtypeStruct((2, 2, 2, 256, 640), BF16),
            jax.ShapeDtypeStruct((2, 2, 2, 256, 256), BF16),
        ],
        in_specs=[spec(SM)] * 3 + [spec(VM)] * 2,
        out_specs=[spec(VM)] * 2,
        scratch_shapes=[VM((16, 10, 64, 64), F32)],
        compiler_params=params(),
    )(meta, coupling_cols, coupling_len, coupling_vals, dense)
    west, east, left = lax.optimization_barrier((west, east, left))
    at_west = shift(east, "px", 1)
    at_east = shift(west, "px", -1)
    at_west, at_east = lax.optimization_barrier((at_west, at_east))

    ints = lambda n: jax.ShapeDtypeStruct((n,), jnp.int32)
    deliver, extra, source, plain, ids, pick = pl.pallas_call(
        route_kernel,
        out_shape=[ints(16 * 32), ints(64), ints(32), ints(32), ints(32), ints(8)],
        in_specs=[spec(SM)] * 2,
        out_specs=[spec(SM)] * 6,
        scratch_shapes=[SM((16,), jnp.int32)],
    )(meta, owner_map.reshape(64))
    branch = pick
    for flip in (1, 2, 4):
        other = lax.ppermute(branch, "px", [(x, x ^ flip) for x in range(size_x)])
        branch = jnp.maximum(branch, other)

    def galerkin(ax, side, outs, spaces, *extra_args):
        half = lambda *shape: pl.BlockSpec((1,) + shape, lambda n: (ax,) + (0,) * len(shape))
        return pl.pallas_call(
            lambda *refs: galerkin_kernel(ax, *refs),
            grid=(1,),
            out_shape=outs,
            in_specs=[half(2, 2, 256, 640), half(2, 2, 256, 256)]
            + [spec(VM)] * (4 + len(extra_args)),
            out_specs=spaces,
            scratch_shapes=([] if ax else [VM((3, 64, 1600), F32)])
            + [
                VM((24, 64, 256), BF16),
                VM((24, 64, 256), BF16),
                VM((256, 1024), F32),
            ],
            compiler_params=params(),
        )(left, turned, dense, side, at_south, at_north, *extra_args)

    row = jax.ShapeDtypeStruct((3, 64, 1600), F32)
    packed = jax.ShapeDtypeStruct((16, 2, 8, 2176), F32)
    send, part = galerkin(
        1, at_east, [jax.ShapeDtypeStruct((3, 64, 1280), F32), row], [spec(VM)] * 2
    )
    got = shift(send, "px", 1)
    own, packed1 = galerkin(0, at_west, [row, packed], [spec(VM)] * 2, part)
    packed2 = pl.pallas_call(
        pack_kernel,
        grid=(1,),
        out_shape=packed,
        in_specs=[spec(VM)] * 2 + [spec(pl.ANY)],
        out_specs=pl.BlockSpec((16, 1, 8, 2176), lambda n: (0, 0, 0, 0)),
        scratch_shapes=[VM((3, 64, 1600), F32)],
        input_output_aliases={2: 0},
        compiler_params=params(),
    )(own, got, packed1)
    spread = lax.all_to_all(packed2, "py", 0, 0, tiled=True)
    branches = [
        lambda a, most=most: relay(KEPT, most, meta, deliver, extra, source, a) for most in SPARES
    ]
    branches.append(lambda a: relay(32, 0, meta, deliver, extra, plain, a))
    rows = lax.switch(branch[0], branches, spread)
    return rows, ids


def solution(mesh):
    in_specs = (
        P("px", "py", None, None, None),
        P("px", "py", None),
        P("px", "py"),
        P("px", "py", None, None, None),
        P("px", "py", None),
        P("px", "py"),
        P("px", None, None, None),
    )
    out_specs = (P(("px", "py"), None, None, None), P(("px", "py")))
    return jax.shard_map(body, mesh=mesh, in_specs=in_specs, out_specs=out_specs, check_vma=False)
```

time: 257 us -> 199 us (0.77)
  waiting for transfers between devices: 101 us -> 63 us
  starting transfers between devices: 36.9 us -> 25 us
  blocking collectives: 48.8 us -> 43.2 us
    all_gather x1, waiting for transfers between devices: 57.1 us -> 33 us  [relay(): far = lax.all_gather(fan[1], 'py', axis=0, tiled=False)]
    ppermute x12 -> x8, waiting for transfers between devices: 34.3 us -> 17.8 us  [the longest x5 11.9 us: shift(): return lax.ppermute(value, axis, pairs)]
    ppermute x12 -> x8, starting transfers between devices: 32.6 us -> 19.4 us  [the longest x5 15.5 us: shift(): return lax.ppermute(value, axis, pairs)]
    all_to_all x1, blocking collectives: 48.8 us -> 43.2 us  [relay(): near = lax.all_to_all(fan[0], 'py', 0, 0, tiled=True)]
    pallas_call x4 -> x7, Pallas kernels: 42.5 us -> 39.9 us  [the longest x2 14.5 us: collect(): pl.pallas_call(lambda *refs: collect_kernel(low, high, base is None, *ref...]
  transfers between devices with their start and end apart: 14 -> 10, of which waited for: 9 -> 8; matrix products, arithmetic and copies ran while one was open for 1% -> 1% of each run, Pallas kernels for 2% -> 14%
where the time goes in v2:
time: 199 us; the launch traced here: 197 us
  waiting for transfers between devices  63 us (32%)
  Pallas kernels  47.7 us (24%)
  blocking collectives  43.2 us (22%)
  starting transfers between devices  25 us (13%)
  between operations  14.2 us (7%)
  local copies, waits for them, and re-layouts  3.47 us (2%)
    all_to_all x1, blocking collectives, relay(): near = lax.all_to_all(fan[0], 'py', 0, 0, tiled=True)  43.2 us
    all_gather x1, waiting for transfers between devices, relay(): far = lax.all_gather(fan[1], 'py', axis=0, tiled=False)  33 us
    ppermute x5, starting transfers between devices, shift(): return lax.ppermute(value, axis, pairs)  15.5 us
    pallas_call x2, Pallas kernels, collect(): pl.pallas_call(lambda *refs: collect_kernel(low, high, base is None, *ref...  14.5 us
    pallas_call x2, Pallas kernels, galerkin(): pl.pallas_call(lambda *refs: galerkin_kernel(ax, *refs), grid=(1,), out_s...  12.3 us
    all_to_all x1, waiting for transfers between devices, body(): spread = lax.all_to_all(packed2, 'py', 0, 0, tiled=True)  12.3 us
    ppermute x5, waiting for transfers between devices, shift(): return lax.ppermute(value, axis, pairs)  11.9 us
    pallas_call x1, Pallas kernels, body(): pl.pallas_call(prepare_kernel, out_shape=[jax.ShapeDtypeStruct((2, 2, 2,...  7.42 us
  transfers between devices with their start and end apart: 10, of which 8 were waited for; matrix products, arithmetic and copies ran while one was open for 1% of the time, Pallas kernels for 14%

profile of v2, /device:TPU:13, one launch (start us, length us, event | category | flops | bytes accessed | tf_op | source)
XLA Modules:
  0.0 197.4 jit_solution(2995465860523598933)
XLA Ops:
  7.2 4.1 %shard_map.87 = (f32[16,64,256]{2,1,0:T(8,128)}, f32[4,64,256]{2,1,0:T(8,128)}, f32[4,64,256]{2,1,0:T(8,128)}) custom-call(s32[3]{0:T(128)S(1)} %pad_add_fusion.meta, s32[4,4,4]{2,1,0:T(4,128)} %cols.2, s32[4,4]{1,0:T(4,128)} %lens.2, f32[4,4,4,64,64]{4,3,2,1,0:T(8,128)} %vals.2), custom_call_target="tpu_custom_call" | custom-call | tf_op jit(solution)/shard_map/pallas_call | solution.py:438
  11.4 3.5 %collective-permute-start.3 = (f32[4,64,256]{2,1,0:T(8,128)}, f32[4,64,256]{2,1,0:T(8,128)S(1)}, u32[]{:S(2)}, u32[]{:S(2)}) collective-permute-start(f32[4,64,256]{2,1,0:T(8,128)} %get-tuple-element.114), channel_id=1, source_target_pairs={{0,1},{1,2},{2,3},{3,4},{4,5},{5,6},{6,7},{7,8},{8,9},{9,10},{10,1... | collective-permute-start | bytes 786440 | tf_op jit(solution)/shard_map/ppermute | solution.py:450
  14.9 4.0 %collective-permute-start.4 = (f32[4,64,256]{2,1,0:T(8,128)}, f32[4,64,256]{2,1,0:T(8,128)S(1)}, u32[]{:S(2)}, u32[]{:S(2)}) collective-permute-start(f32[4,64,256]{2,1,0:T(8,128)} %get-tuple-element.116), channel_id=1, source_target_pairs={{1,0},{2,1},{3,2},{4,3},{5,4},{6,5},{7,6},{8,7},{9,8},{10,9},{11,1... | collective-permute-start | bytes 786440 | tf_op jit(solution)/shard_map/ppermute | solution.py:450
  20.0 7.4 %shard_map.88 = (bf16[2,2,2,256,640]{4,3,2,1,0:T(8,128)(2,1)}, bf16[2,2,2,256,256]{4,3,2,1,0:T(8,128)(2,1)}) custom-call(s32[3]{0:T(128)S(1)} %pad_add_fusion.meta, s32[4,4,9]{2,1,0:T(4,128)} %cols.3, s32[4,4]{1,0:T(4,128)} %lens.3, f32[4,4,9,64,64]{4,3,2,1,0:T(8,128)} %vals.3, f32[16,64,256]{2,1,0:T(8,128)} %get-tuple-element.115.dense.refs_2_), custom_call_target="tpu_custom_call" | custom-call | tf_op jit(solution)/shard_map/pallas_call | solution.py:456
  27.5 4.2 %collective-permute-start.5 = (f32[6,64,256]{2,1,0:T(8,128)S(1)}, f32[6,64,256]{2,1,0:T(8,128)S(1)}, u32[]{:S(2)}, u32[]{:S(2)}) collective-permute-start(f32[6,64,256]{2,1,0:T(8,128)S(1)} %get-tuple-element.120), channel_id=1, source_target_pairs={{0,16},{16,32},{32,48},{48,64},{64,80},{80,96},{96,112},{1,17},{17... | collective-permute-start | bytes 1179656 | tf_op jit(solution)/shard_map/ppermute | solution.py:450
  31.7 1.9 collective-permute-start.6
  33.6 2.8 %collective-permute-done.5.refs_3_ = f32[6,64,256]{2,1,0:T(8,128)S(1)} collective-permute-done((f32[6,64,256]{2,1,0:T(8,128)S(1)}, f32[6,64,256]{2,1,0:T(8,128)S(1)}, u32[]{:S(2)}, u32[]{:S(2)}) %collective-permute-start.5) | collective-permute-done | bytes 393248 | tf_op jit(solution)/shard_map/ppermute | solution.py:450
  36.4 4.4 %collective-permute-done.6.refs_3_ = f32[6,64,256]{2,1,0:T(8,128)S(1)} collective-permute-done((f32[6,64,256]{2,1,0:T(8,128)S(1)}, f32[6,64,256]{2,1,0:T(8,128)S(1)}, u32[]{:S(2)}, u32[]{:S(2)}) %collective-permute-start.6) | collective-permute-done | bytes 393248 | tf_op jit(solution)/shard_map/ppermute | solution.py:450
  41.6 5.7 %shard_map.89 = (f32[3,64,1280]{2,1,0:T(8,128)}, f32[3,64,1600]{2,1,0:T(8,128)}) custom-call(bf16[2,2,2,256,640]{4,3,2,1,0:T(8,128)(2,1)} %get-tuple-element.118.refs_0_, bf16[2,2,2,256,256]{4,3,2,1,0:T(8,128)(2,1)} %get-tuple-element.119.refs_1_, f32[16,64,256]{2,1,0:T(8,128)} %get-tuple-element.115.dense.refs_2_, f32[6,64,256]{2,1,0:T(8,128)} %copy-done.4, ...), custom_call_target="tpu_custom_call" | custom-call | tf_op jit(solution)/shard_map/pallas_call | solution.py:487
  49.2 6.6 %shard_map.90 = (f32[3,64,1600]{2,1,0:T(8,128)}, f32[16,2,8,2176]{3,2,1,0:T(8,128)}) custom-call(bf16[2,2,2,256,640]{4,3,2,1,0:T(8,128)(2,1)} %get-tuple-element.118.refs_0_, bf16[2,2,2,256,256]{4,3,2,1,0:T(8,128)(2,1)} %get-tuple-element.119.refs_1_, f32[16,64,256]{2,1,0:T(8,128)} %get-tuple-element.115.dense.refs_2_, f32[6,64,256]{2,1,0:T(8,128)} %copy-done.3, ...), custom_call_target="tpu_custom_call" | custom-call | tf_op jit(solution)/shard_map/pallas_call | solution.py:487
  55.8 4.7 %collective-permute-done.7.got = f32[3,64,1280]{2,1,0:T(8,128)S(1)} collective-permute-done((f32[3,64,1280]{2,1,0:T(8,128)}, f32[3,64,1280]{2,1,0:T(8,128)S(1)}, u32[]{:S(2)}, u32[]{:S(2)}) %collective-permute-start.7) | collective-permute-done | bytes 983072 | tf_op jit(solution)/shard_map/ppermute | solution.py:450
  61.4 2.8 %shard_map.91 = f32[16,2,8,2176]{3,2,1,0:T(8,128)} custom-call(f32[3,64,1600]{2,1,0:T(8,128)} %get-tuple-element.125.own, f32[3,64,1280]{2,1,0:T(8,128)} %copy-done.2, f32[16,2,8,2176]{3,2,1,0:T(8,128)} %get-tuple-element.127.packed), custom_call_target="tpu_custom_call", output_to_operand_aliasing={{}: (2, {})} | custom-call | tf_op jit(solution)/shard_map/pallas_call | solution.py:510
  64.3 5.6 %all-to-all-start.5 = ((f32[16,2,8,2176]{3,2,1,0:T(8,128)}), f32[16,2,8,2176]{3,2,1,0:T(8,128)S(1)}, u32[]{:S(2)}, u32[]{:S(2)}) async-start(f32[16,2,8,2176]{3,2,1,0:T(8,128)} %shard_map.91), calls=%async_computation.5 | async-start | bytes 4456448 | tf_op jit(solution)/shard_map/all_to_all | solution.py:520
  70.6 2.8 %shard_map.86 = (s32[512]{0:T(512)S(1)}, s32[64]{0:T(128)S(1)}, s32[32]{0:T(128)S(1)}, s32[32]{0:T(128)S(1)}, s32[32]{0:T(128)}, /*index=5*/s32[8]{0:T(128)}) custom-call(s32[3]{0:T(128)S(1)} %pad_add_fusion.meta, s32[64]{0:T(128)} %reshape.10.owners), custom_call_target="tpu_custom_call" | custom-call | tf_op jit(solution)/shard_map/pallas_call | solution.py:473
  76.8 2.7 %collective-permute-done.1 = s32[8]{0:T(128)S(1)} collective-permute-done((s32[8]{0:T(128)S(1)}, s32[8]{0:T(128)S(1)}, u32[]{:S(2)}, u32[]{:S(2)}) %collective-permute-start.1) | collective-permute-done | bytes 64 | tf_op jit(solution)/shard_map/ppermute | solution.py:482
  79.5 2.0 %collective-permute-start.2 = (s32[8]{0:T(128)S(1)}, s32[8]{0:T(128)S(1)}, u32[]{:S(2)}, u32[]{:S(2)}) collective-permute-start(s32[8]{0:T(128)S(1)} %max.10), channel_id=1, source_target_pairs={{0,64},{16,80},{32,96},{48,112},{64,0},{80,16},{96,32},{112,48},{1... | collective-permute-start | bytes 104 | tf_op jit(solution)/shard_map/ppermute | solution.py:482
  81.5 2.2 %collective-permute-done.2 = s32[8]{0:T(128)S(1)} collective-permute-done((s32[8]{0:T(128)S(1)}, s32[8]{0:T(128)S(1)}, u32[]{:S(2)}, u32[]{:S(2)}) %collective-permute-start.2) | collective-permute-done | bytes 64 | tf_op jit(solution)/shard_map/ppermute | solution.py:482
  83.8 12.3 %all-to-all-done.5 = f32[16,2,8,2176]{3,2,1,0:T(8,128)S(1)} async-done(((f32[16,2,8,2176]{3,2,1,0:T(8,128)}), f32[16,2,8,2176]{3,2,1,0:T(8,128)S(1)}, u32[]{:S(2)}, u32[]{:S(2)}) %all-to-all-start.5) | async-done | bytes 2228256 | tf_op jit(solution)/shard_map/all_to_all | solution.py:520
  96.0 94.5 %conditional.1 = (f32[32,25,64,64]{3,2,1,0:T(8,128)}) conditional(s32[]{:T(128)} %bitcast.6, (s32[3]{0:T(128)S(1)}, s32[512]{0:T(512)S(1)}, s32[64]{0:T(128)S(1)}, f32[16,2,8,2176]{3,2,1,0:T(8,128)S(1)}, s32[32]{0:T(128)S(1)}) %tuple.27, (s32[3]{0:T(128)S(1)}, s32[512]{0:T(512)S(1)}, s32[64]{0:T(128)S(1)}, ...), branch_computations={%region_0.0_spmd, %region_1.0_spmd, %region_2.0_spmd, %region_3.0_... | conditional | bytes 34983984 | solution.py:525
  96.0 3.8 %branch_2_fun.3 = (f32[16,3,8,1664]{3,2,1,0:T(8,128)}, f32[9,8,1664]{2,1,0:T(8,128)}) custom-call(s32[3]{0:T(128)S(1)} %get-tuple-element.71.refs_0_, s32[512]{0:T(512)S(1)} %get-tuple-element.72.refs_1_, s32[64]{0:T(128)S(1)} %get-tuple-element.73.refs_2_, f32[16,2,8,2176]{3,2,1,0:T(8,128)S(1)} %get-tuple-element.74.refs_3_), custom_call_target="tpu_custom_call" | custom-call | tf_op jit(solution)/shard_map/cond/branch_2_fun/pallas_call | solution.py:412
  99.8 43.2 %all_to_all.27.refs_1_ = f32[16,3,8,1664]{3,2,1,0:T(8,128)} all-to-all(f32[16,3,8,1664]{3,2,1,0:T(8,128)} %get-tuple-element.76), channel_id=1, replica_groups=mesh['px'=8,'py'=16] {'py'}, dimensions={0} | all-to-all | bytes 5111808 | tf_op jit(solution)/shard_map/cond/branch_2_fun/all_to_all | solution.py:422
  143.0 10.7 %branch_2_fun.4.refs_2_ = f32[32,25,64,64]{3,2,1,0:T(8,128)} custom-call(s32[32]{0:T(128)S(1)} %get-tuple-element.70.refs_0_, f32[16,3,8,1664]{3,2,1,0:T(8,128)} %all_to_all.27.refs_1_), custom_call_target="tpu_custom_call" | custom-call | tf_op jit(solution)/shard_map/cond/branch_2_fun/pallas_call | solution.py:393
  153.8 33.0 %all-gather.13.cloned.1.call-done = f32[144,8,1664]{2,1,0:T(8,128)} async-done(((f32[9,8,1664]{2,1,0:T(8,128)}), f32[144,8,1664]{2,1,0:T(8,128)}) %all-gather.13.cloned.1.call-update) | async-done | bytes 7667728 | tf_op jit(solution)/shard_map/cond/branch_2_fun/all_gather | solution.py:421
  186.8 3.8 %branch_2_fun.5 = f32[32,25,64,64]{3,2,1,0:T(8,128)} custom-call(s32[32]{0:T(128)S(1)} %get-tuple-element.70.refs_0_, f32[16,9,8,1664]{3,2,1,0:T(8,128)} %bitcast.13, f32[32,25,64,64]{3,2,1,0:T(8,128)} %branch_2_fun.4.refs_2_), custom_call_target="tpu_custom_call", output_to_operand_aliasing={{}: (2, {})} | custom-call | tf_op jit(solution)/shard_map/cond/branch_2_fun/pallas_call | solution.py:393
  (30 shorter events, 9.0 us)
Async XLA Ops:
  11.4 16.1 %collective-permute-start.3 = (f32[4,64,256]{2,1,0:T(8,128)}, f32[4,64,256]{2,1,0:T(8,128)S(1)}, u32[]{:S(2)}, u32[]{:S(2)}) collective-permute-start(f32[4,64,256]{2,1,0:T(8,128)} %get-tuple-element.114), channel_id=1, source_target_pairs={{0,1},{1,2},{2,3},{3,4},{4,5},{5,6},{6,7},{7,8},{8,9},{9,10},{10,1... | collective-permute-start | bytes 786440 | tf_op jit(solution)/shard_map/ppermute | solution.py:450
  14.9 12.5 %collective-permute-start.4 = (f32[4,64,256]{2,1,0:T(8,128)}, f32[4,64,256]{2,1,0:T(8,128)S(1)}, u32[]{:S(2)}, u32[]{:S(2)}) collective-permute-start(f32[4,64,256]{2,1,0:T(8,128)} %get-tuple-element.116), channel_id=1, source_target_pairs={{1,0},{2,1},{3,2},{4,3},{5,4},{6,5},{7,6},{8,7},{9,8},{10,9},{11,1... | collective-permute-start | bytes 786440 | tf_op jit(solution)/shard_map/ppermute | solution.py:450
  27.4 13.4 %copy-start = (f32[4,64,256]{2,1,0:T(8,128)}, f32[4,64,256]{2,1,0:T(8,128)S(1)}, u32[]{:S(2)}) copy-start(f32[4,64,256]{2,1,0:T(8,128)S(1)} %collective-permute-done.3.refs_4_) | copy-start | bytes 786436
  27.5 13.4 %copy-start.1 = (f32[4,64,256]{2,1,0:T(8,128)}, f32[4,64,256]{2,1,0:T(8,128)S(1)}, u32[]{:S(2)}) copy-start(f32[4,64,256]{2,1,0:T(8,128)S(1)} %collective-permute-done.4.refs_5_) | copy-start | bytes 786436
  27.5 8.9 %collective-permute-start.5 = (f32[6,64,256]{2,1,0:T(8,128)S(1)}, f32[6,64,256]{2,1,0:T(8,128)S(1)}, u32[]{:S(2)}, u32[]{:S(2)}) collective-permute-start(f32[6,64,256]{2,1,0:T(8,128)S(1)} %get-tuple-element.120), channel_id=1, source_target_pairs={{0,16},{16,32},{32,48},{48,64},{64,80},{80,96},{96,112},{1,17},{17... | collective-permute-start | bytes 1179656 | tf_op jit(solution)/shard_map/ppermute | solution.py:450
  31.7 9.1 %collective-permute-start.6 = (f32[6,64,256]{2,1,0:T(8,128)S(1)}, f32[6,64,256]{2,1,0:T(8,128)S(1)}, u32[]{:S(2)}, u32[]{:S(2)}) collective-permute-start(f32[6,64,256]{2,1,0:T(8,128)S(1)} %get-tuple-element.121), channel_id=1, source_target_pairs={{16,0},{32,16},{48,32},{64,48},{80,64},{96,80},{112,96},{17,1},{33... | collective-permute-start | bytes 1179656 | tf_op jit(solution)/shard_map/ppermute | solution.py:450
  36.4 12.7 %copy-start.3 = (f32[6,64,256]{2,1,0:T(8,128)}, f32[6,64,256]{2,1,0:T(8,128)S(1)}, u32[]{:S(2)}) copy-start(f32[6,64,256]{2,1,0:T(8,128)S(1)} %collective-permute-done.5.refs_3_) | copy-start | bytes 1179652
  40.8 0.7 copy-start.4
  47.2 13.3 %collective-permute-start.7 = (f32[3,64,1280]{2,1,0:T(8,128)}, f32[3,64,1280]{2,1,0:T(8,128)S(1)}, u32[]{:S(2)}, u32[]{:S(2)}) collective-permute-start(f32[3,64,1280]{2,1,0:T(8,128)} %get-tuple-element.126), channel_id=1, source_target_pairs={{0,16},{16,32},{32,48},{48,64},{64,80},{80,96},{96,112},{1,17},{17... | collective-permute-start | bytes 2949128 | tf_op jit(solution)/shard_map/ppermute | solution.py:450
  55.8 14.1 %copy-start.5 = (s32[1,16,4,1]{1,3,2,0:T(1,128)S(1)}, s32[1,16,4,1]{1,3,2,0:T(1,128)}, u32[]{:S(2)}) copy-start(s32[1,16,4,1]{1,3,2,0:T(1,128)} %param.18) | copy-start | bytes 772
  60.5 0.9 copy-start.2
  64.3 31.7 %all-to-all-start.5 = ((f32[16,2,8,2176]{3,2,1,0:T(8,128)}), f32[16,2,8,2176]{3,2,1,0:T(8,128)S(1)}, u32[]{:S(2)}, u32[]{:S(2)}) async-start(f32[16,2,8,2176]{3,2,1,0:T(8,128)} %shard_map.91), calls=%async_computation.5 | async-start | bytes 4456448 | tf_op jit(solution)/shard_map/all_to_all | solution.py:520
  73.4 2.9 %collective-permute-start = (s32[8]{0:T(128)}, s32[8]{0:T(128)S(1)}, u32[]{:S(2)}, u32[]{:S(2)}) collective-permute-start(s32[8]{0:T(128)} %get-tuple-element.111), channel_id=1, source_target_pairs={{0,16},{16,0},{32,48},{48,32},{64,80},{80,64},{96,112},{112,96},{1... | collective-permute-start | bytes 104 | tf_op jit(solution)/shard_map/ppermute | solution.py:482
  76.8 2.7 %collective-permute-start.1 = (s32[8]{0:T(128)S(1)}, s32[8]{0:T(128)S(1)}, u32[]{:S(2)}, u32[]{:S(2)}) collective-permute-start(s32[8]{0:T(128)S(1)} %max.9), channel_id=1, source_target_pairs={{0,32},{16,48},{32,0},{48,16},{64,96},{80,112},{96,64},{112,80},{1... | collective-permute-start | bytes 104 | tf_op jit(solution)/shard_map/ppermute | solution.py:482
  79.5 4.2 %collective-permute-start.2 = (s32[8]{0:T(128)S(1)}, s32[8]{0:T(128)S(1)}, u32[]{:S(2)}, u32[]{:S(2)}) collective-permute-start(s32[8]{0:T(128)S(1)} %max.10), channel_id=1, source_target_pairs={{0,64},{16,80},{32,96},{48,112},{64,0},{80,16},{96,32},{112,48},{1... | collective-permute-start | bytes 104 | tf_op jit(solution)/shard_map/ppermute | solution.py:482
  96.0 90.7 %all-gather.13.cloned.1.call-start = ((), (), s32[]{:S(2)}) async-start(), calls=%async_computation.8 | async-start | bytes 8146944 | tf_op jit(solution)/shard_map/cond/branch_2_fun/all_gather | solution.py:421
Sparse Core Ops, SparseCore 0:
  99.9 86.7 all-gather.12

commit v3 on v2

--- a/solution.py
+++ b/solution.py
@@ -8,6 +8,7 @@
 KEPT = 6
 SPARES = (14, 16, 18, 22)
 BUFFERS = 4
+STARTS = (-256, 1024, 2304)
 VM = pltpu.VMEM
 SM = pltpu.SMEM
 F32 = jnp.float32
@@ -174,8 +175,8 @@
                     piece = coarse[rows, ty * 256 : ty * 256 + 256]
                     at = ((ty + 1 - qy) * 5 + 1 - qx) * 64
                     if ax == 1 and qx == 1:
-                        at = (ty + 1 - qy) * 256
-                        send[ay + qy, :, at : at + 256] += piece
+                        at = STARTS[ay + qy] + (ty + 1 - qy) * 256
+                        send[:, at : at + 256] += piece
                     elif ax == 1:
                         part[ay + qy, :, at : at + 256] += piece
                     elif qx == 1:
@@ -208,8 +209,9 @@
 def pack_kernel(own, got, packed, out, acc):
     for iy in range(3):
         acc[iy] = own[iy]
-        for jy in range(5):
-            acc[iy, :, jy * 320 : jy * 320 + 256] += got[iy, :, jy * 256 : jy * 256 + 256]
+        for jy in range(iy == 0, 5 - (iy == 2)):
+            at = STARTS[iy] + jy * 256
+            acc[iy, :, jy * 320 : jy * 320 + 256] += got[:, at : at + 256]
     pack_rows([acc[iy] for iy in range(3)], out, 0)
 
 
@@ -503,7 +505,7 @@
     row = jax.ShapeDtypeStruct((3, 64, 1600), F32)
     packed = jax.ShapeDtypeStruct((16, 2, 8, 2176), F32)
     send, part = galerkin(
-        1, at_east, [jax.ShapeDtypeStruct((3, 64, 1280), F32), row], [spec(VM)] * 2
+        1, at_east, [jax.ShapeDtypeStruct((64, 3328), F32), row], [spec(VM)] * 2
     )
     got = shift(send, "px", 1)
     own, packed1 = galerkin(0, at_west, [row, packed], [spec(VM)] * 2, part)

time: 199 us -> 198 us (level)
  transfers between devices with their start and end apart: 10 -> 10, of which waited for: 8 -> 8; matrix products, arithmetic and copies ran while one was open for 1% -> 1% of each run, Pallas kernels for 14% -> 12%
where the time goes in v3:
time: 198 us; the launch traced here: 196 us
  waiting for transfers between devices  62.2 us (31%)
  Pallas kernels  48.1 us (24%)
  blocking collectives  42.4 us (21%)
  starting transfers between devices  25 us (13%)
  between operations  14.2 us (7%)
  local copies, waits for them, and re-layouts  3.42 us (2%)
    all_to_all x1, blocking collectives, relay(): near = lax.all_to_all(fan[0], 'py', 0, 0, tiled=True)  42.4 us
    all_gather x1, waiting for transfers between devices, relay(): far = lax.all_gather(fan[1], 'py', axis=0, tiled=False)  33.5 us
    ppermute x5, starting transfers between devices, shift(): return lax.ppermute(value, axis, pairs)  15.5 us
    pallas_call x2, Pallas kernels, collect(): pl.pallas_call(lambda *refs: collect_kernel(low, high, base is None, *ref...  15 us
    all_to_all x1, waiting for transfers between devices, body(): spread = lax.all_to_all(packed2, 'py', 0, 0, tiled=True)  12.2 us
    pallas_call x2, Pallas kernels, galerkin(): pl.pallas_call(lambda *refs: galerkin_kernel(ax, *refs), grid=(1,), out_s...  12.2 us
    ppermute x5, waiting for transfers between devices, shift(): return lax.ppermute(value, axis, pairs)  10.5 us
    pallas_call x1, Pallas kernels, body(): pl.pallas_call(prepare_kernel, out_shape=[jax.ShapeDtypeStruct((2, 2, 2,...  7.42 us
  transfers between devices with their start and end apart: 10, of which 8 were waited for; matrix products, arithmetic and copies ran while one was open for 1% of the time, Pallas kernels for 12%

profile of v3, /device:TPU:13, one launch (start us, length us, event | category | flops | bytes accessed | tf_op | source)
XLA Modules:
  0.0 196.2 jit_solution(14463333578703059712)
XLA Ops:
  7.2 4.1 %shard_map.87 = (f32[16,64,256]{2,1,0:T(8,128)}, f32[4,64,256]{2,1,0:T(8,128)}, f32[4,64,256]{2,1,0:T(8,128)}) custom-call(s32[3]{0:T(128)S(1)} %pad_add_fusion.meta, s32[4,4,4]{2,1,0:T(4,128)} %cols.2, s32[4,4]{1,0:T(4,128)} %lens.2, f32[4,4,4,64,64]{4,3,2,1,0:T(8,128)} %vals.2), custom_call_target="tpu_custom_call" | custom-call | tf_op jit(solution)/shard_map/pallas_call | solution.py:440
  11.4 3.5 %collective-permute-start.3 = (f32[4,64,256]{2,1,0:T(8,128)}, f32[4,64,256]{2,1,0:T(8,128)S(1)}, u32[]{:S(2)}, u32[]{:S(2)}) collective-permute-start(f32[4,64,256]{2,1,0:T(8,128)} %get-tuple-element.114), channel_id=1, source_target_pairs={{0,1},{1,2},{2,3},{3,4},{4,5},{5,6},{6,7},{7,8},{8,9},{9,10},{10,1... | collective-permute-start | bytes 786440 | tf_op jit(solution)/shard_map/ppermute | solution.py:452
  14.9 4.0 %collective-permute-start.4 = (f32[4,64,256]{2,1,0:T(8,128)}, f32[4,64,256]{2,1,0:T(8,128)S(1)}, u32[]{:S(2)}, u32[]{:S(2)}) collective-permute-start(f32[4,64,256]{2,1,0:T(8,128)} %get-tuple-element.116), channel_id=1, source_target_pairs={{1,0},{2,1},{3,2},{4,3},{5,4},{6,5},{7,6},{8,7},{9,8},{10,9},{11,1... | collective-permute-start | bytes 786440 | tf_op jit(solution)/shard_map/ppermute | solution.py:452
  20.0 7.4 %shard_map.88 = (bf16[2,2,2,256,640]{4,3,2,1,0:T(8,128)(2,1)}, bf16[2,2,2,256,256]{4,3,2,1,0:T(8,128)(2,1)}) custom-call(s32[3]{0:T(128)S(1)} %pad_add_fusion.meta, s32[4,4,9]{2,1,0:T(4,128)} %cols.3, s32[4,4]{1,0:T(4,128)} %lens.3, f32[4,4,9,64,64]{4,3,2,1,0:T(8,128)} %vals.3, f32[16,64,256]{2,1,0:T(8,128)} %get-tuple-element.115.dense.refs_2_), custom_call_target="tpu_custom_call" | custom-call | tf_op jit(solution)/shard_map/pallas_call | solution.py:458
  27.5 4.2 %collective-permute-start.5 = (f32[6,64,256]{2,1,0:T(8,128)S(1)}, f32[6,64,256]{2,1,0:T(8,128)S(1)}, u32[]{:S(2)}, u32[]{:S(2)}) collective-permute-start(f32[6,64,256]{2,1,0:T(8,128)S(1)} %get-tuple-element.120), channel_id=1, source_target_pairs={{0,16},{16,32},{32,48},{48,64},{64,80},{80,96},{96,112},{1,17},{17... | collective-permute-start | bytes 1179656 | tf_op jit(solution)/shard_map/ppermute | solution.py:452
  31.7 1.9 collective-permute-start.6
  33.6 2.8 %collective-permute-done.5.refs_3_ = f32[6,64,256]{2,1,0:T(8,128)S(1)} collective-permute-done((f32[6,64,256]{2,1,0:T(8,128)S(1)}, f32[6,64,256]{2,1,0:T(8,128)S(1)}, u32[]{:S(2)}, u32[]{:S(2)}) %collective-permute-start.5) | collective-permute-done | bytes 393248 | tf_op jit(solution)/shard_map/ppermute | solution.py:452
  36.4 4.4 %collective-permute-done.6.refs_3_ = f32[6,64,256]{2,1,0:T(8,128)S(1)} collective-permute-done((f32[6,64,256]{2,1,0:T(8,128)S(1)}, f32[6,64,256]{2,1,0:T(8,128)S(1)}, u32[]{:S(2)}, u32[]{:S(2)}) %collective-permute-start.6) | collective-permute-done | bytes 393248 | tf_op jit(solution)/shard_map/ppermute | solution.py:452
  41.6 5.6 %shard_map.89 = (f32[64,3328]{1,0:T(8,128)}, f32[3,64,1600]{2,1,0:T(8,128)}) custom-call(bf16[2,2,2,256,640]{4,3,2,1,0:T(8,128)(2,1)} %get-tuple-element.118.refs_0_, bf16[2,2,2,256,256]{4,3,2,1,0:T(8,128)(2,1)} %get-tuple-element.119.refs_1_, f32[16,64,256]{2,1,0:T(8,128)} %get-tuple-element.115.dense.refs_2_, f32[6,64,256]{2,1,0:T(8,128)} %copy-done.4, ...), custom_call_target="tpu_custom_call" | custom-call | tf_op jit(solution)/shard_map/pallas_call | solution.py:489
  49.1 6.6 %shard_map.90 = (f32[3,64,1600]{2,1,0:T(8,128)}, f32[16,2,8,2176]{3,2,1,0:T(8,128)}) custom-call(bf16[2,2,2,256,640]{4,3,2,1,0:T(8,128)(2,1)} %get-tuple-element.118.refs_0_, bf16[2,2,2,256,256]{4,3,2,1,0:T(8,128)(2,1)} %get-tuple-element.119.refs_1_, f32[16,64,256]{2,1,0:T(8,128)} %get-tuple-element.115.dense.refs_2_, f32[6,64,256]{2,1,0:T(8,128)} %copy-done.3, ...), custom_call_target="tpu_custom_call" | custom-call | tf_op jit(solution)/shard_map/pallas_call | solution.py:489
  55.7 3.3 %collective-permute-done.7.got = f32[64,3328]{1,0:T(8,128)S(1)} collective-permute-done((f32[64,3328]{1,0:T(8,128)}, f32[64,3328]{1,0:T(8,128)S(1)}, u32[]{:S(2)}, u32[]{:S(2)}) %collective-permute-start.7) | collective-permute-done | bytes 852000 | tf_op jit(solution)/shard_map/ppermute | solution.py:452
  59.9 2.8 %shard_map.91 = f32[16,2,8,2176]{3,2,1,0:T(8,128)} custom-call(f32[3,64,1600]{2,1,0:T(8,128)} %get-tuple-element.125.own, f32[64,3328]{1,0:T(8,128)} %copy-done.2, f32[16,2,8,2176]{3,2,1,0:T(8,128)} %get-tuple-element.127.packed), custom_call_target="tpu_custom_call", output_to_operand_aliasing={{}: (2, {})} | custom-call | tf_op jit(solution)/shard_map/pallas_call | solution.py:512
  62.7 5.6 %all-to-all-start.5 = ((f32[16,2,8,2176]{3,2,1,0:T(8,128)}), f32[16,2,8,2176]{3,2,1,0:T(8,128)S(1)}, u32[]{:S(2)}, u32[]{:S(2)}) async-start(f32[16,2,8,2176]{3,2,1,0:T(8,128)} %shard_map.91), calls=%async_computation.5 | async-start | bytes 4456448 | tf_op jit(solution)/shard_map/all_to_all | solution.py:522
  69.0 2.8 %shard_map.86 = (s32[512]{0:T(512)S(1)}, s32[64]{0:T(128)S(1)}, s32[32]{0:T(128)S(1)}, s32[32]{0:T(128)S(1)}, s32[32]{0:T(128)}, /*index=5*/s32[8]{0:T(128)}) custom-call(s32[3]{0:T(128)S(1)} %pad_add_fusion.meta, s32[64]{0:T(128)} %reshape.10.owners), custom_call_target="tpu_custom_call" | custom-call | tf_op jit(solution)/shard_map/pallas_call | solution.py:475
  75.3 2.7 %collective-permute-done.1 = s32[8]{0:T(128)S(1)} collective-permute-done((s32[8]{0:T(128)S(1)}, s32[8]{0:T(128)S(1)}, u32[]{:S(2)}, u32[]{:S(2)}) %collective-permute-start.1) | collective-permute-done | bytes 64 | tf_op jit(solution)/shard_map/ppermute | solution.py:484
  78.0 2.0 %collective-permute-start.2 = (s32[8]{0:T(128)S(1)}, s32[8]{0:T(128)S(1)}, u32[]{:S(2)}, u32[]{:S(2)}) collective-permute-start(s32[8]{0:T(128)S(1)} %max.10), channel_id=1, source_target_pairs={{0,64},{16,80},{32,96},{48,112},{64,0},{80,16},{96,32},{112,48},{1... | collective-permute-start | bytes 104 | tf_op jit(solution)/shard_map/ppermute | solution.py:484
  80.0 2.2 %collective-permute-done.2 = s32[8]{0:T(128)S(1)} collective-permute-done((s32[8]{0:T(128)S(1)}, s32[8]{0:T(128)S(1)}, u32[]{:S(2)}, u32[]{:S(2)}) %collective-permute-start.2) | collective-permute-done | bytes 64 | tf_op jit(solution)/shard_map/ppermute | solution.py:484
  82.2 12.2 %all-to-all-done.5 = f32[16,2,8,2176]{3,2,1,0:T(8,128)S(1)} async-done(((f32[16,2,8,2176]{3,2,1,0:T(8,128)}), f32[16,2,8,2176]{3,2,1,0:T(8,128)S(1)}, u32[]{:S(2)}, u32[]{:S(2)}) %all-to-all-start.5) | async-done | bytes 2228256 | tf_op jit(solution)/shard_map/all_to_all | solution.py:522
  94.5 94.9 %conditional.1 = (f32[32,25,64,64]{3,2,1,0:T(8,128)}) conditional(s32[]{:T(128)} %bitcast.6, (s32[3]{0:T(128)S(1)}, s32[512]{0:T(512)S(1)}, s32[64]{0:T(128)S(1)}, f32[16,2,8,2176]{3,2,1,0:T(8,128)S(1)}, s32[32]{0:T(128)S(1)}) %tuple.27, (s32[3]{0:T(128)S(1)}, s32[512]{0:T(512)S(1)}, s32[64]{0:T(128)S(1)}, ...), branch_computations={%region_0.0_spmd, %region_1.0_spmd, %region_2.0_spmd, %region_3.0_... | conditional | bytes 34983984 | solution.py:527
  94.5 3.7 %branch_1_fun.3 = (f32[16,3,8,1664]{3,2,1,0:T(8,128)}, f32[8,8,1664]{2,1,0:T(8,128)}) custom-call(s32[3]{0:T(128)S(1)} %get-tuple-element.64.refs_0_, s32[512]{0:T(512)S(1)} %get-tuple-element.65.refs_1_, s32[64]{0:T(128)S(1)} %get-tuple-element.66.refs_2_, f32[16,2,8,2176]{3,2,1,0:T(8,128)S(1)} %get-tuple-element.67.refs_3_), custom_call_target="tpu_custom_call" | custom-call | tf_op jit(solution)/shard_map/cond/branch_1_fun/pallas_call | solution.py:414
  98.2 42.4 %all_to_all.26.refs_1_ = f32[16,3,8,1664]{3,2,1,0:T(8,128)} all-to-all(f32[16,3,8,1664]{3,2,1,0:T(8,128)} %get-tuple-element.69), channel_id=1, replica_groups=mesh['px'=8,'py'=16] {'py'}, dimensions={0} | all-to-all | bytes 5111808 | tf_op jit(solution)/shard_map/cond/branch_1_fun/all_to_all | solution.py:424
  140.6 6.8 %branch_1_fun.4.refs_2_ = f32[32,25,64,64]{3,2,1,0:T(8,128)} custom-call(s32[32]{0:T(128)S(1)} %get-tuple-element.63.refs_0_, f32[16,3,8,1664]{3,2,1,0:T(8,128)} %all_to_all.26.refs_1_), custom_call_target="tpu_custom_call" | custom-call | tf_op jit(solution)/shard_map/cond/branch_1_fun/pallas_call | solution.py:395
  147.4 33.5 %all-gather.11.cloned.1.call-done = f32[128,8,1664]{2,1,0:T(8,128)} async-done(((f32[8,8,1664]{2,1,0:T(8,128)}), f32[128,8,1664]{2,1,0:T(8,128)}) %all-gather.11.cloned.1.call-update) | async-done | bytes 6815760 | tf_op jit(solution)/shard_map/cond/branch_1_fun/all_gather | solution.py:423
  180.9 8.3 %branch_1_fun.5 = f32[32,25,64,64]{3,2,1,0:T(8,128)} custom-call(s32[32]{0:T(128)S(1)} %get-tuple-element.63.refs_0_, f32[16,8,8,1664]{3,2,1,0:T(8,128)} %bitcast.14, f32[32,25,64,64]{3,2,1,0:T(8,128)} %branch_1_fun.4.refs_2_), custom_call_target="tpu_custom_call", output_to_operand_aliasing={{}: (2, {})} | custom-call | tf_op jit(solution)/shard_map/cond/branch_1_fun/pallas_call | solution.py:395
  (30 shorter events, 9.0 us)
Async XLA Ops:
  11.4 16.1 %collective-permute-start.3 = (f32[4,64,256]{2,1,0:T(8,128)}, f32[4,64,256]{2,1,0:T(8,128)S(1)}, u32[]{:S(2)}, u32[]{:S(2)}) collective-permute-start(f32[4,64,256]{2,1,0:T(8,128)} %get-tuple-element.114), channel_id=1, source_target_pairs={{0,1},{1,2},{2,3},{3,4},{4,5},{5,6},{6,7},{7,8},{8,9},{9,10},{10,1... | collective-permute-start | bytes 786440 | tf_op jit(solution)/shard_map/ppermute | solution.py:452
  14.9 12.5 %collective-permute-start.4 = (f32[4,64,256]{2,1,0:T(8,128)}, f32[4,64,256]{2,1,0:T(8,128)S(1)}, u32[]{:S(2)}, u32[]{:S(2)}) collective-permute-start(f32[4,64,256]{2,1,0:T(8,128)} %get-tuple-element.116), channel_id=1, source_target_pairs={{1,0},{2,1},{3,2},{4,3},{5,4},{6,5},{7,6},{8,7},{9,8},{10,9},{11,1... | collective-permute-start | bytes 786440 | tf_op jit(solution)/shard_map/ppermute | solution.py:452
  27.4 13.4 %copy-start = (f32[4,64,256]{2,1,0:T(8,128)}, f32[4,64,256]{2,1,0:T(8,128)S(1)}, u32[]{:S(2)}) copy-start(f32[4,64,256]{2,1,0:T(8,128)S(1)} %collective-permute-done.3.refs_4_) | copy-start | bytes 786436
  27.5 13.4 %copy-start.1 = (f32[4,64,256]{2,1,0:T(8,128)}, f32[4,64,256]{2,1,0:T(8,128)S(1)}, u32[]{:S(2)}) copy-start(f32[4,64,256]{2,1,0:T(8,128)S(1)} %collective-permute-done.4.refs_5_) | copy-start | bytes 786436
  27.5 8.9 %collective-permute-start.5 = (f32[6,64,256]{2,1,0:T(8,128)S(1)}, f32[6,64,256]{2,1,0:T(8,128)S(1)}, u32[]{:S(2)}, u32[]{:S(2)}) collective-permute-start(f32[6,64,256]{2,1,0:T(8,128)S(1)} %get-tuple-element.120), channel_id=1, source_target_pairs={{0,16},{16,32},{32,48},{48,64},{64,80},{80,96},{96,112},{1,17},{17... | collective-permute-start | bytes 1179656 | tf_op jit(solution)/shard_map/ppermute | solution.py:452
  31.7 9.1 %collective-permute-start.6 = (f32[6,64,256]{2,1,0:T(8,128)S(1)}, f32[6,64,256]{2,1,0:T(8,128)S(1)}, u32[]{:S(2)}, u32[]{:S(2)}) collective-permute-start(f32[6,64,256]{2,1,0:T(8,128)S(1)} %get-tuple-element.121), channel_id=1, source_target_pairs={{16,0},{32,16},{48,32},{64,48},{80,64},{96,80},{112,96},{17,1},{33... | collective-permute-start | bytes 1179656 | tf_op jit(solution)/shard_map/ppermute | solution.py:452
  36.4 12.7 %copy-start.3 = (f32[6,64,256]{2,1,0:T(8,128)}, f32[6,64,256]{2,1,0:T(8,128)S(1)}, u32[]{:S(2)}) copy-start(f32[6,64,256]{2,1,0:T(8,128)S(1)} %collective-permute-done.5.refs_3_) | copy-start | bytes 1179652
  40.8 0.7 copy-start.4
  47.2 11.8 %collective-permute-start.7 = (f32[64,3328]{1,0:T(8,128)}, f32[64,3328]{1,0:T(8,128)S(1)}, u32[]{:S(2)}, u32[]{:S(2)}) collective-permute-start(f32[64,3328]{1,0:T(8,128)} %get-tuple-element.126), channel_id=1, source_target_pairs={{0,16},{16,32},{32,48},{48,64},{64,80},{80,96},{96,112},{1,17},{17... | collective-permute-start | bytes 2555912 | tf_op jit(solution)/shard_map/ppermute | solution.py:452
  55.7 12.6 %copy-start.5 = (s32[1,16,4,1]{1,3,2,0:T(1,128)S(1)}, s32[1,16,4,1]{1,3,2,0:T(1,128)}, u32[]{:S(2)}) copy-start(s32[1,16,4,1]{1,3,2,0:T(1,128)} %param.18) | copy-start | bytes 772
  59.0 0.9 copy-start.2
  62.7 31.7 %all-to-all-start.5 = ((f32[16,2,8,2176]{3,2,1,0:T(8,128)}), f32[16,2,8,2176]{3,2,1,0:T(8,128)S(1)}, u32[]{:S(2)}, u32[]{:S(2)}) async-start(f32[16,2,8,2176]{3,2,1,0:T(8,128)} %shard_map.91), calls=%async_computation.5 | async-start | bytes 4456448 | tf_op jit(solution)/shard_map/all_to_all | solution.py:522
  71.8 2.9 %collective-permute-start = (s32[8]{0:T(128)}, s32[8]{0:T(128)S(1)}, u32[]{:S(2)}, u32[]{:S(2)}) collective-permute-start(s32[8]{0:T(128)} %get-tuple-element.111), channel_id=1, source_target_pairs={{0,16},{16,0},{32,48},{48,32},{64,80},{80,64},{96,112},{112,96},{1... | collective-permute-start | bytes 104 | tf_op jit(solution)/shard_map/ppermute | solution.py:484
  75.3 2.7 %collective-permute-start.1 = (s32[8]{0:T(128)S(1)}, s32[8]{0:T(128)S(1)}, u32[]{:S(2)}, u32[]{:S(2)}) collective-permute-start(s32[8]{0:T(128)S(1)} %max.9), channel_id=1, source_target_pairs={{0,32},{16,48},{32,0},{48,16},{64,96},{80,112},{96,64},{112,80},{1... | collective-permute-start | bytes 104 | tf_op jit(solution)/shard_map/ppermute | solution.py:484
  78.0 4.2 %collective-permute-start.2 = (s32[8]{0:T(128)S(1)}, s32[8]{0:T(128)S(1)}, u32[]{:S(2)}, u32[]{:S(2)}) collective-permute-start(s32[8]{0:T(128)S(1)} %max.10), channel_id=1, source_target_pairs={{0,64},{16,80},{32,96},{48,112},{64,0},{80,16},{96,32},{112,48},{1... | collective-permute-start | bytes 104 | tf_op jit(solution)/shard_map/ppermute | solution.py:484
  94.5 86.5 %all-gather.11.cloned.1.call-start = ((), (), s32[]{:S(2)}) async-start(), calls=%async_computation.7 | async-start | bytes 7241728 | tf_op jit(solution)/shard_map/cond/branch_1_fun/all_gather | solution.py:423
Sparse Core Ops, SparseCore 0:
  98.3 82.5 all-gather.10
